TPU v7x, 512 devices: a whole 4x4x16 slice. The times are simulated.
512 devices in a mesh: rows: 64 (over z, x_hi, core), cols: 8 (over y, x_lo).
Axes of the slice: x: 4 (x_hi: 2, x_lo: 2; x = x_hi * 2 + x_lo), y: 4, z: 16, core: 2. Of those that a mesh axis runs over, the one named last changes fastest.
Arguments:
- atmosphere_variables: bfloat16 [2, 512, 256, 512], P(None, 'rows', 'cols'), may hold values from -24 to 24
- premix_gain_vector: float32 [512], replicated, may hold values from 0.5 to 1.5
- expand_weight: bfloat16 [512, 1024], replicated, may hold values from -0.25 to 0.25
- depth_weight: float32 [3, 3, 1024], replicated, may hold values from -2 to 2
- depth_bias: float32 [1024], replicated, may hold values from -3 to 3
- project_weight: bfloat16 [1024, 512], replicated, may hold values from -0.1875 to 0.1875
- norm_attn: float32 [512], replicated, may hold values from 0.5 to 1.5
- qkv_weight: bfloat16 [512, 1536], replicated, may hold values from -0.25 to 0.25
- out_weight: bfloat16 [512, 512], replicated, may hold values from -0.25 to 0.25
- bias_table: float32 [16, 15, 15], replicated, may hold values from -2 to 310
Outputs:
- mixed_fields: bfloat16 [2, 512, 256, 512], P(None, 'rows', 'cols')
All inputs are finite; a program needn't handle non-finite values.
Results may differ from a plain program's by a relative error of at most 0.0052.
Values may be sent and summed in bfloat16 or wider, within the bound.
A program may use at most 64 MiB of HBM per device.

v0:
```python
import jax
import jax.numpy as jnp
from jax import lax
from jax.sharding import PartitionSpec as P


def extended(x, sides, width):
    for axis, dim in sides:
        devices, length = (lax.axis_size(axis), x.shape[dim])
        up = [(i, (i + 1) % devices) for i in range(devices - 1)]
        down = [(j, i) for i, j in up]
        last = lax.slice_in_dim(x, length - width, length, axis=dim)
        first = lax.slice_in_dim(x, 0, width, axis=dim)
        before = lax.ppermute(last, axis, up)
        after = lax.ppermute(first, axis, down)
        x = jnp.concatenate([before, x, after], axis=dim)
    return x


def passed_along(x, axis, by):
    devices = lax.axis_size(axis)
    return lax.ppermute(x, axis, [(i, (i + by) % devices) for i in range(devices)])


def normalize_channels(values, gain_vector):
    average = jnp.mean(values, axis=-1, keepdims=True)
    centred = values - average
    variance = jnp.mean(centred * centred, axis=-1, keepdims=True)
    return centred * lax.rsqrt(variance + 1e-05) * gain_vector


def expand_tokens(tile_fields, premix_gain_vector, expand_weight):
    tile_shape = tile_fields.shape
    standardized = normalize_channels(tile_fields.astype(jnp.float32), premix_gain_vector).astype(
        jnp.bfloat16
    )
    product = jnp.dot(
        standardized.reshape(-1, tile_shape[-1]), expand_weight, preferred_element_type=jnp.float32
    )
    return (
        jax.nn.gelu(product)
        .astype(jnp.bfloat16)
        .reshape(tile_shape[:-1] + (expand_weight.shape[1],))
    )


def relative_bias(bias_table):
    head_count = bias_table.shape[0]
    table_span = bias_table.shape[1]
    grid_side = (table_span + 1) // 2
    position = jnp.arange(grid_side * grid_side)
    row_of = position // grid_side
    col_of = position % grid_side
    flat_code = (row_of[:, None] - row_of[None, :] + grid_side - 1) * table_span
    flat_code = flat_code + (col_of[:, None] - col_of[None, :] + grid_side - 1)
    one_hot = (flat_code[:, :, None] == jnp.arange(table_span * table_span)[None, None, :]).astype(
        jnp.float32
    )
    return jnp.einsum(
        "ijc,hc->hij",
        one_hot,
        bias_table.reshape(head_count, table_span * table_span),
        precision=lax.Precision.HIGHEST,
    )


def grid_attention(groups, qkv_weight, position_bias):
    group_count, member_count, embedding_dimension = groups.shape
    head_count = position_bias.shape[0]
    head_size = embedding_dimension // head_count
    projected = jnp.dot(
        groups.reshape(-1, embedding_dimension), qkv_weight, preferred_element_type=jnp.float32
    )
    projected = projected.astype(jnp.bfloat16).reshape(
        group_count, member_count, 3, head_count, head_size
    )
    scores = jnp.einsum(
        "gihd,gjhd->ghij",
        projected[:, :, 0],
        projected[:, :, 1],
        preferred_element_type=jnp.float32,
    )
    scores = scores * head_size ** (-0.5) + position_bias[None]
    attention = jax.nn.softmax(scores, axis=-1).astype(jnp.bfloat16)
    context = jnp.einsum(
        "ghij,gjhd->gihd", attention, projected[:, :, 2], preferred_element_type=jnp.float32
    )
    return context.astype(jnp.bfloat16).reshape(group_count, member_count, embedding_dimension)


def on_device(
    atmosphere_variables,
    premix_gain_vector,
    expand_weight,
    depth_weight,
    depth_bias,
    project_weight,
    norm_attn,
    qkv_weight,
    out_weight,
    bias_table,
):
    prediction_results, patch_northward, patch_eastward, embedding_dimension = (
        atmosphere_variables.shape
    )
    expanded_channel_breadth = expand_weight.shape[1]
    expanded = expand_tokens(atmosphere_variables, premix_gain_vector, expand_weight)
    padded = extended(expanded, (("rows", 1), ("cols", 2)), 1)
    filtered_fields = jnp.zeros(
        (prediction_results, patch_northward, patch_eastward, expanded_channel_breadth), jnp.float32
    )
    for row_tap in range(3):
        for col_tap in range(3):
            window = padded[
                :, row_tap : row_tap + patch_northward, col_tap : col_tap + patch_eastward, :
            ]
            filtered_fields = (
                filtered_fields + window.astype(jnp.float32) * depth_weight[row_tap, col_tap]
            )
    activated = jax.nn.gelu(filtered_fields + depth_bias).astype(jnp.bfloat16)
    residual_path = jnp.dot(
        activated.reshape(-1, expanded_channel_breadth),
        project_weight,
        preferred_element_type=jnp.float32,
    )
    convolution_result = (
        atmosphere_variables.reshape(-1, embedding_dimension).astype(jnp.float32) + residual_path
    ).astype(jnp.bfloat16)
    attention_input = normalize_channels(convolution_result.astype(jnp.float32), norm_attn).astype(
        jnp.bfloat16
    )
    col_count = lax.axis_size("cols")
    eastward_offset_patch = 8 // col_count
    lattice_eastward = patch_eastward // eastward_offset_patch
    grid_index_rows = attention_input.reshape(
        prediction_results,
        patch_northward,
        eastward_offset_patch,
        lattice_eastward,
        embedding_dimension,
    )
    grid_index_rows = grid_index_rows.transpose(0, 1, 3, 2, 4).reshape(
        -1, eastward_offset_patch, embedding_dimension
    )
    gid_total = grid_index_rows.shape[0]
    per_owner = gid_total // 8
    per_device = per_owner // col_count
    member = lax.axis_index("rows") // col_count
    owner_pieces = grid_index_rows.reshape(8, per_owner, eastward_offset_patch, embedding_dimension)
    received = [lax.dynamic_index_in_dim(owner_pieces, member, 0, keepdims=False)]
    for offset in range(1, 8):
        outgoing = lax.dynamic_index_in_dim(owner_pieces, (member + offset) % 8, 0, keepdims=False)
        received.append(passed_along(outgoing, "rows", offset * col_count))
    stacked = jnp.stack(received)
    by_member = jnp.take(stacked, (member - jnp.arange(8)) % 8, axis=0)
    sectioned = by_member.reshape(
        8, col_count, 1, per_device, eastward_offset_patch, embedding_dimension
    )
    gathered = lax.all_to_all(sectioned, "cols", split_axis=1, concat_axis=2, tiled=True)
    groups = gathered.reshape(8, col_count, per_device, eastward_offset_patch, embedding_dimension)
    groups = groups.transpose(2, 0, 1, 3, 4).reshape(per_device, 64, embedding_dimension)
    context = grid_attention(groups, qkv_weight, relative_bias(bias_table))
    returning = context.reshape(
        per_device, 8, col_count, eastward_offset_patch, embedding_dimension
    ).transpose(1, 2, 0, 3, 4)
    returning = returning.reshape(
        8, 1, col_count, per_device, eastward_offset_patch, embedding_dimension
    )
    returned = lax.all_to_all(returning, "cols", split_axis=2, concat_axis=1, tiled=True)
    member = lax.axis_index("rows") // col_count
    member_pieces = returned.reshape(8, per_owner, eastward_offset_patch, embedding_dimension)
    coming = [lax.dynamic_index_in_dim(member_pieces, member, 0, keepdims=False)]
    for offset in range(1, 8):
        outgoing = lax.dynamic_index_in_dim(member_pieces, (member + offset) % 8, 0, keepdims=False)
        coming.append(passed_along(outgoing, "rows", offset * col_count))
    stacked_back = jnp.stack(coming)
    by_owner = jnp.take(stacked_back, (member - jnp.arange(8)) % 8, axis=0)
    grid_index_back = by_owner.reshape(gid_total, eastward_offset_patch, embedding_dimension)
    tile_context_window = grid_index_back.reshape(
        prediction_results,
        patch_northward,
        lattice_eastward,
        eastward_offset_patch,
        embedding_dimension,
    )
    tile_context_window = tile_context_window.transpose(0, 1, 3, 2, 4).reshape(
        -1, embedding_dimension
    )
    attn_out = jnp.dot(tile_context_window, out_weight, preferred_element_type=jnp.float32)
    blended_elements = (convolution_result.astype(jnp.float32) + attn_out).astype(jnp.bfloat16)
    return blended_elements.reshape(
        prediction_results, patch_northward, patch_eastward, embedding_dimension
    )


def solution(mesh):
    return jax.shard_map(
        on_device,
        mesh=mesh,
        in_specs=(P(None, "rows", "cols", None), P(), P(), P(), P(), P(), P(), P(), P(), P()),
        out_specs=P(None, "rows", "cols", None),
        check_vma=False,
    )
```

profile of v0, /device:TPU:34, one launch (start us, length us, event | category | flops | bytes accessed | tf_op | source)
XLA Modules:
  0.0 206.3 jit_solution(995356407925264242)
XLA Ops:
  7.2 6.0 %collective-permute-start.1 = (bf16[2,1,32,1024]{3,2,1,0:T(8,128)(2,1)S(1)}, bf16[2,1,32,1024]{3,2,1,0:T(8,128)(2,1)S(1)}, u32[]{:S(2)}, u32[]{:S(2)}) collective-permute-start(bf16[2,1,32,1024]{3,2,1,0:T(8,128)(2,1)S(1)} %get-tuple-element.14), channel_id=1, source_target_pairs={{8,0},{16,8},{24,16},{32,24},{40,32},{48,40},{56,48},{64,56},{72,6... | collective-permute-start | bytes 393224 | tf_op jit(solution)/shard_map/ppermute | solution.py:15
  15.9 3.5 %collective-permute-start.2 = (bf16[2,10,1,1024]{3,2,1,0:T(2,128)(2,1)S(1)}, bf16[2,10,1,1024]{3,2,1,0:T(2,128)(2,1)S(1)}, u32[]{:S(2)}, u32[]{:S(2)}) collective-permute-start(bf16[2,10,1,1024]{3,2,1,0:T(2,128)(2,1)S(1)} %get-tuple-element.11), channel_id=1, source_target_pairs={{0,1},{1,2},{2,3},{3,4},{4,5},{5,6},{6,7},{8,9},{9,10},{10,11},{11... | collective-permute-start | bytes 122888 | tf_op jit(solution)/shard_map/ppermute | solution.py:14
  19.4 2.4 %collective-permute-start.3 = (bf16[2,10,1,1024]{3,2,1,0:T(2,128)(2,1)S(1)}, bf16[2,10,1,1024]{3,2,1,0:T(2,128)(2,1)S(1)}, u32[]{:S(2)}, u32[]{:S(2)}) collective-permute-start(bf16[2,10,1,1024]{3,2,1,0:T(2,128)(2,1)S(1)} %get-tuple-element.12), channel_id=1, source_target_pairs={{1,0},{2,1},{3,2},{4,3},{5,4},{6,5},{7,6},{9,8},{10,9},{11,10},{12... | collective-permute-start | bytes 122888 | tf_op jit(solution)/shard_map/ppermute | solution.py:15
  22.7 3.9 %collective-permute-done.3 = bf16[2,10,1,1024]{3,2,1,0:T(2,128)(2,1)S(1)} collective-permute-done((bf16[2,10,1,1024]{3,2,1,0:T(2,128)(2,1)S(1)}, bf16[2,10,1,1024]{3,2,1,0:T(2,128)(2,1)S(1)}, u32[]{:S(2)}, u32[]{:S(2)}) %collective-permute-start.3) | collective-permute-done | bytes 40992 | tf_op jit(solution)/shard_map/ppermute | solution.py:15
  27.4 3.3 %fusion.18 = bf16[2,8,32,1024]{3,2,1,0:T(8,128)(2,1)S(1)} fusion(bf16[2,8,32,1024]{3,2,1,0:T(8,128)(2,1)S(1)} %bitcast.137, bf16[2,10,33,1024]{3,2,1,0:T(8,128)(2,1)S(1)} %get-tuple-element.10, bf16[2,1,32,1024]{3,2,1,0:T(8,128)(2,1)S(1)} %collective-permute-done.1, bf16[2,10,33,1024]{3,2,1,0:T(8,128)(2,1)S(1)} %get-tuple-element.9, ...), kind=kLoop, calls=%fused_computation.27 | loop fusion | flops 19922944 | bytes 8691712 | tf_op jit(solution)/shard_map/convert_element_type | solution.py:120
  32.2 5.2 %collective-permute-start.4 = (bf16[64,1,512]{2,0,1:T(8,128)(2,1)S(1)}, bf16[64,1,512]{2,0,1:T(8,128)(2,1)S(1)}, u32[]{:S(2)}, u32[]{:S(2)}) collective-permute-start(bf16[64,1,512]{2,0,1:T(8,128)(2,1)S(1)} %get-tuple-element.29), channel_id=1, source_target_pairs={{0,64},{8,72},{16,80},{24,88},{32,96},{40,104},{48,112},{56,120},{... | collective-permute-start | bytes 196616 | tf_op jit(solution)/shard_map/ppermute | solution.py:22
  37.4 7.7 %collective-permute-start.10 = (bf16[64,1,512]{2,0,1:T(8,128)(2,1)S(1)}, bf16[64,1,512]{2,0,1:T(8,128)(2,1)S(1)}, u32[]{:S(2)}, u32[]{:S(2)}) collective-permute-start(bf16[64,1,512]{2,0,1:T(8,128)(2,1)S(1)} %get-tuple-element.23), channel_id=1, source_target_pairs={{0,448},{8,456},{16,464},{24,472},{32,480},{40,488},{48,496},{56,5... | collective-permute-start | bytes 196616 | tf_op jit(solution)/shard_map/ppermute | solution.py:22
  45.1 6.9 %collective-permute-start.9 = (bf16[64,1,512]{2,0,1:T(8,128)(2,1)S(1)}, bf16[64,1,512]{2,0,1:T(8,128)(2,1)S(1)}, u32[]{:S(2)}, u32[]{:S(2)}) collective-permute-start(bf16[64,1,512]{2,0,1:T(8,128)(2,1)S(1)} %get-tuple-element.24), channel_id=1, source_target_pairs={{0,384},{8,392},{16,400},{24,408},{32,416},{40,424},{48,432},{56,4... | collective-permute-start | bytes 196616 | tf_op jit(solution)/shard_map/ppermute | solution.py:22
  52.0 4.9 %collective-permute-start.8 = (bf16[64,1,512]{2,0,1:T(8,128)(2,1)S(1)}, bf16[64,1,512]{2,0,1:T(8,128)(2,1)S(1)}, u32[]{:S(2)}, u32[]{:S(2)}) collective-permute-start(bf16[64,1,512]{2,0,1:T(8,128)(2,1)S(1)} %get-tuple-element.25), channel_id=1, source_target_pairs={{0,320},{8,328},{16,336},{24,344},{32,352},{40,360},{48,368},{56,3... | collective-permute-start | bytes 196616 | tf_op jit(solution)/shard_map/ppermute | solution.py:22
  56.9 7.5 %collective-permute-start.7 = (bf16[64,1,512]{2,0,1:T(8,128)(2,1)S(1)}, bf16[64,1,512]{2,0,1:T(8,128)(2,1)S(1)}, u32[]{:S(2)}, u32[]{:S(2)}) collective-permute-start(bf16[64,1,512]{2,0,1:T(8,128)(2,1)S(1)} %get-tuple-element.26), channel_id=1, source_target_pairs={{0,256},{8,264},{16,272},{24,280},{32,288},{40,296},{48,304},{56,3... | collective-permute-start | bytes 196616 | tf_op jit(solution)/shard_map/ppermute | solution.py:22
  64.5 2.2 %collective-permute-start.5 = (bf16[64,1,512]{2,0,1:T(8,128)(2,1)S(1)}, bf16[64,1,512]{2,0,1:T(8,128)(2,1)S(1)}, u32[]{:S(2)}, u32[]{:S(2)}) collective-permute-start(bf16[64,1,512]{2,0,1:T(8,128)(2,1)S(1)} %get-tuple-element.28), channel_id=1, source_target_pairs={{0,128},{8,136},{16,144},{24,152},{32,160},{40,168},{48,176},{56,1... | collective-permute-start | bytes 196616 | tf_op jit(solution)/shard_map/ppermute | solution.py:22
  66.7 13.6 %collective-permute-done.5 = bf16[64,1,512]{2,0,1:T(8,128)(2,1)S(1)} collective-permute-done((bf16[64,1,512]{2,0,1:T(8,128)(2,1)S(1)}, bf16[64,1,512]{2,0,1:T(8,128)(2,1)S(1)}, u32[]{:S(2)}, u32[]{:S(2)}) %collective-permute-start.5) | collective-permute-done | bytes 65568 | tf_op jit(solution)/shard_map/ppermute | solution.py:22
  80.3 3.9 %collective-permute-start.6 = (bf16[64,1,512]{2,0,1:T(8,128)(2,1)S(1)}, bf16[64,1,512]{2,0,1:T(8,128)(2,1)S(1)}, u32[]{:S(2)}, u32[]{:S(2)}) collective-permute-start(bf16[64,1,512]{2,0,1:T(8,128)(2,1)S(1)} %get-tuple-element.27), channel_id=1, source_target_pairs={{0,192},{8,200},{16,208},{24,216},{32,224},{40,232},{48,240},{56,2... | collective-permute-start | bytes 196616 | tf_op jit(solution)/shard_map/ppermute | solution.py:22
  84.3 14.6 %collective-permute-done.6 = bf16[64,1,512]{2,0,1:T(8,128)(2,1)S(1)} collective-permute-done((bf16[64,1,512]{2,0,1:T(8,128)(2,1)S(1)}, bf16[64,1,512]{2,0,1:T(8,128)(2,1)S(1)}, u32[]{:S(2)}, u32[]{:S(2)}) %collective-permute-start.6) | collective-permute-done | bytes 65568 | tf_op jit(solution)/shard_map/ppermute | solution.py:22
  102.4 5.7 %all-to-all-start = ((bf16[8,8,1,8,1,512]{5,3,0,4,2,1:T(8,128)(2,1)}), bf16[8,8,1,8,1,512]{5,3,0,4,2,1:T(8,128)(2,1)S(1)}, u32[]{:S(2)}, u32[]{:S(2)}) async-start(bf16[8,8,1,8,1,512]{5,3,0,4,2,1:T(8,128)(2,1)} %copy.49), calls=%async_computation | async-start | bytes 1048576 | tf_op jit(solution)/shard_map/all_to_all | solution.py:159
  108.1 3.6 %fusion.29 = f32[16,64,64]{2,0,1:T(8,128)} fusion(f32[16,225,1]{1,0,2:T(8,128)S(1)} %reshape.236, s32[64,64]{1,0:T(8,128)S(1)} %add_add_fusion), kind=kOutput, calls=%fused_computation.44 | convolution fusion | flops 177868800 | bytes 292928 | tf_op jit(solution)/shard_map/ijc,hc->hij/dot_general | solution.py:59
  112.9 4.1 %all-to-all-done = bf16[8,8,1,8,1,512]{5,3,0,4,2,1:T(8,128)(2,1)S(1)} async-done(((bf16[8,8,1,8,1,512]{5,3,0,4,2,1:T(8,128)(2,1)}), bf16[8,8,1,8,1,512]{5,3,0,4,2,1:T(8,128)(2,1)S(1)}, u32[]{:S(2)}, u32[]{:S(2)}) %all-to-all-start) | async-done | bytes 524320 | tf_op jit(solution)/shard_map/all_to_all | solution.py:159
  117.3 2.2 %convolution_convert_fusion = bf16[512,1536]{1,0:T(8,128)(2,1)} fusion(bf16[512,512]{1,0:T(8,128)(2,1)S(1)} %bitcast.147, bf16[512,1536]{1,0:T(8,128)(2,1)S(1)} %copy-done), kind=kOutput, calls=%fused_computation.11 | convolution fusion | flops 806092800 | bytes 3670016 | tf_op jit(solution)/shard_map/dot_general | solution.py:71
  119.5 2.6 %copy.51 = bf16[512,1536]{0,1:T(8,128)(2,1)} copy(bf16[512,1536]{1,0:T(8,128)(2,1)} %convolution_convert_fusion) | data formatting | bytes 3145728 | tf_op jit(solution)/shard_map/convert_element_type | solution.py:74
  122.1 5.1 %reshape.200 = bf16[8,64,3,16,32]{1,0,4,3,2:T(8,128)(2,1)} reshape(bf16[512,1536]{0,1:T(8,128)(2,1)} %copy.51) | data formatting | bytes 3145728 | tf_op jit(solution)/shard_map/reshape | solution.py:74
  127.2 2.1 %fusion.37 = (bf16[8,64,1,16,32]{1,0,4,3,2:T(8,128)(2,1)S(1)}, bf16[8,64,1,16,32]{1,0,4,3,2:T(8,128)(2,1)S(1)}, bf16[8,64,1,16,32]{1,0,4,3,2:T(8,128)(2,1)S(1)}) fusion(bf16[8,64,3,16,32]{1,0,4,3,2:T(8,128)(2,1)} %reshape.200), kind=kLoop, calls=%fused_computation.112 | loop fusion | bytes 3145728 | tf_op jit(solution)/shard_map/slice | solution.py:86
  133.6 3.5 %copy.58 = bf16[8,64,16,32]{3,2,1,0:T(8,128)(2,1)} copy(bf16[8,64,16,32]{1,3,2,0:T(8,128)(2,1)} %fusion.24) | data formatting | bytes 1048576 | tf_op jit(solution)/shard_map/convert_element_type | solution.py:88
  137.1 3.4 %reshape_reshape.7 = bf16[8,8,8,1,512]{4,2,1,0,3:T(8,128)(2,1)S(1)} reshape(bf16[8,64,16,32]{3,2,1,0:T(8,128)(2,1)} %copy.58) | data formatting | bytes 1048576 | tf_op jit(solution)/shard_map/reshape;reshape | solution.py:163
  140.6 11.7 %all_to_all.8 = bf16[8,1,8,8,1,512]{5,0,3,4,1,2:T(8,128)(2,1)S(1)} all-to-all(bf16[8,1,8,8,1,512]{5,0,3,4,1,2:T(8,128)(2,1)S(1)} %copy.59), channel_id=1, replica_groups=mesh['rows'=64,'cols'=8] {'cols'}, dimensions={2} | all-to-all | bytes 1048576 | tf_op jit(solution)/shard_map/all_to_all | solution.py:169
  154.5 6.0 %collective-permute-start.17 = (bf16[64,1,512]{2,0,1:T(8,128)(2,1)S(1)}, bf16[64,1,512]{2,0,1:T(8,128)(2,1)S(1)}, u32[]{:S(2)}, u32[]{:S(2)}) collective-permute-start(bf16[64,1,512]{2,0,1:T(8,128)(2,1)S(1)} %get-tuple-element.15), channel_id=1, source_target_pairs={{0,448},{8,456},{16,464},{24,472},{32,480},{40,488},{48,496},{56,5... | collective-permute-start | bytes 196616 | tf_op jit(solution)/shard_map/ppermute | solution.py:22
  162.4 4.0 %collective-permute-start.15 = (bf16[64,1,512]{2,0,1:T(8,128)(2,1)S(1)}, bf16[64,1,512]{2,0,1:T(8,128)(2,1)S(1)}, u32[]{:S(2)}, u32[]{:S(2)}) collective-permute-start(bf16[64,1,512]{2,0,1:T(8,128)(2,1)S(1)} %get-tuple-element.17), channel_id=1, source_target_pairs={{0,320},{8,328},{16,336},{24,344},{32,352},{40,360},{48,368},{56,3... | collective-permute-start | bytes 196616 | tf_op jit(solution)/shard_map/ppermute | solution.py:22
  166.5 10.5 %collective-permute-start.14 = (bf16[64,1,512]{2,0,1:T(8,128)(2,1)S(1)}, bf16[64,1,512]{2,0,1:T(8,128)(2,1)S(1)}, u32[]{:S(2)}, u32[]{:S(2)}) collective-permute-start(bf16[64,1,512]{2,0,1:T(8,128)(2,1)S(1)} %get-tuple-element.18), channel_id=1, source_target_pairs={{0,256},{8,264},{16,272},{24,280},{32,288},{40,296},{48,304},{56,3... | collective-permute-start | bytes 196616 | tf_op jit(solution)/shard_map/ppermute | solution.py:22
  177.0 4.3 %collective-permute-start.12 = (bf16[64,1,512]{2,0,1:T(8,128)(2,1)S(1)}, bf16[64,1,512]{2,0,1:T(8,128)(2,1)S(1)}, u32[]{:S(2)}, u32[]{:S(2)}) collective-permute-start(bf16[64,1,512]{2,0,1:T(8,128)(2,1)S(1)} %get-tuple-element.20), channel_id=1, source_target_pairs={{0,128},{8,136},{16,144},{24,152},{32,160},{40,168},{48,176},{56,1... | collective-permute-start | bytes 196616 | tf_op jit(solution)/shard_map/ppermute | solution.py:22
  181.3 6.6 %collective-permute-done.12 = bf16[64,1,512]{2,0,1:T(8,128)(2,1)S(1)} collective-permute-done((bf16[64,1,512]{2,0,1:T(8,128)(2,1)S(1)}, bf16[64,1,512]{2,0,1:T(8,128)(2,1)S(1)}, u32[]{:S(2)}, u32[]{:S(2)}) %collective-permute-start.12) | collective-permute-done | bytes 65568 | tf_op jit(solution)/shard_map/ppermute | solution.py:22
  187.9 3.5 %collective-permute-start.13 = (bf16[64,1,512]{2,0,1:T(8,128)(2,1)S(1)}, bf16[64,1,512]{2,0,1:T(8,128)(2,1)S(1)}, u32[]{:S(2)}, u32[]{:S(2)}) collective-permute-start(bf16[64,1,512]{2,0,1:T(8,128)(2,1)S(1)} %get-tuple-element.19), channel_id=1, source_target_pairs={{0,192},{8,200},{16,208},{24,216},{32,224},{40,232},{48,240},{56,2... | collective-permute-start | bytes 196616 | tf_op jit(solution)/shard_map/ppermute | solution.py:22
  191.4 10.0 %collective-permute-done.13 = bf16[64,1,512]{2,0,1:T(8,128)(2,1)S(1)} collective-permute-done((bf16[64,1,512]{2,0,1:T(8,128)(2,1)S(1)}, bf16[64,1,512]{2,0,1:T(8,128)(2,1)S(1)}, u32[]{:S(2)}, u32[]{:S(2)}) %collective-permute-start.13) | collective-permute-done | bytes 65568 | tf_op jit(solution)/shard_map/ppermute | solution.py:22
  204.1 2.3 %fusion.26 = bf16[512,512]{1,0:T(8,128)(2,1)} fusion(bf16[512,512]{1,0:T(8,128)(2,1)S(1)} %bitcast.142, bf16[512,512]{1,0:T(8,128)(2,1)} %param.20, bf16[512,512]{1,0:T(8,128)(2,1)S(1)} %get-tuple-element.41), kind=kOutput, calls=%fused_computation.41 | convolution fusion | flops 269221888 | bytes 2097152 | tf_op jit(solution)/shard_map/dot_general | solution.py:189
  (90 shorter events, 28.9 us)
Async XLA Ops:
  0.0 117.3 %copy-start = (bf16[512,1536]{1,0:T(8,128)(2,1)S(1)}, bf16[512,1536]{1,0:T(8,128)(2,1)}, u32[]{:S(2)}) copy-start(bf16[512,1536]{1,0:T(8,128)(2,1)} %param.19) | copy-start | bytes 4718596
  0.0 4.0 %copy-start.10 = (bf16[512,1024]{1,0:T(8,128)(2,1)S(1)}, bf16[512,1024]{1,0:T(8,128)(2,1)}, u32[]{:S(2)}) copy-start(bf16[512,1024]{1,0:T(8,128)(2,1)} %param.14) | copy-start | bytes 3145732
  4.0 9.3 %copy-start.5 = (f32[3,3,1024]{2,1,0:T(4,128)S(1)}, f32[3,3,1024]{2,1,0:T(4,128)}, u32[]{:S(2)}) copy-start(f32[3,3,1024]{2,1,0:T(4,128)} %param.15) | copy-start | bytes 110596
  5.1 17.2 %copy-start.4 = (f32[16,15,15]{2,0,1:T(8,128)S(1)}, f32[16,15,15]{2,0,1:T(8,128)}, u32[]{:S(2)}) copy-start(f32[16,15,15]{2,0,1:T(8,128)} %param.21) | copy-start | bytes 43204
  5.2 8.8 %collective-permute-start = (bf16[2,1,32,1024]{3,2,1,0:T(8,128)(2,1)S(1)}, bf16[2,1,32,1024]{3,2,1,0:T(8,128)(2,1)S(1)}, u32[]{:S(2)}, u32[]{:S(2)}) collective-permute-start(bf16[2,1,32,1024]{3,2,1,0:T(8,128)(2,1)S(1)} %get-tuple-element.13), channel_id=1, source_target_pairs={{0,8},{8,16},{16,24},{24,32},{32,40},{40,48},{48,56},{56,64},{64,7... | collective-permute-start | bytes 393224 | tf_op jit(solution)/shard_map/ppermute | solution.py:14
  7.2 8.6 %collective-permute-start.1 = (bf16[2,1,32,1024]{3,2,1,0:T(8,128)(2,1)S(1)}, bf16[2,1,32,1024]{3,2,1,0:T(8,128)(2,1)S(1)}, u32[]{:S(2)}, u32[]{:S(2)}) collective-permute-start(bf16[2,1,32,1024]{3,2,1,0:T(8,128)(2,1)S(1)} %get-tuple-element.14), channel_id=1, source_target_pairs={{8,0},{16,8},{24,16},{32,24},{40,32},{48,40},{56,48},{64,56},{72,6... | collective-permute-start | bytes 393224 | tf_op jit(solution)/shard_map/ppermute | solution.py:15
  15.9 6.8 %collective-permute-start.2 = (bf16[2,10,1,1024]{3,2,1,0:T(2,128)(2,1)S(1)}, bf16[2,10,1,1024]{3,2,1,0:T(2,128)(2,1)S(1)}, u32[]{:S(2)}, u32[]{:S(2)}) collective-permute-start(bf16[2,10,1,1024]{3,2,1,0:T(2,128)(2,1)S(1)} %get-tuple-element.11), channel_id=1, source_target_pairs={{0,1},{1,2},{2,3},{3,4},{4,5},{5,6},{6,7},{8,9},{9,10},{10,11},{11... | collective-permute-start | bytes 122888 | tf_op jit(solution)/shard_map/ppermute | solution.py:14
  19.4 7.2 %collective-permute-start.3 = (bf16[2,10,1,1024]{3,2,1,0:T(2,128)(2,1)S(1)}, bf16[2,10,1,1024]{3,2,1,0:T(2,128)(2,1)S(1)}, u32[]{:S(2)}, u32[]{:S(2)}) collective-permute-start(bf16[2,10,1,1024]{3,2,1,0:T(2,128)(2,1)S(1)} %get-tuple-element.12), channel_id=1, source_target_pairs={{1,0},{2,1},{3,2},{4,3},{5,4},{6,5},{7,6},{9,8},{10,9},{11,10},{12... | collective-permute-start | bytes 122888 | tf_op jit(solution)/shard_map/ppermute | solution.py:15
  22.6 4.8 %copy-start.6 = (f32[1024]{0:T(1024)S(1)}, f32[1024]{0:T(1024)}, u32[]{:S(2)}) copy-start(f32[1024]{0:T(1024)} %param.16) | copy-start | bytes 12292
  27.4 3.3 %copy-start.1 = (bf16[2,8,32,512]{3,2,1,0:T(8,128)(2,1)S(1)}, bf16[2,8,32,512]{3,2,1,0:T(8,128)(2,1)}, u32[]{:S(2)}) copy-start(bf16[2,8,32,512]{3,2,1,0:T(8,128)(2,1)} %param.12) | copy-start | bytes 1572868
  27.4 3.3 %copy-start.11 = (bf16[1024,512]{1,0:T(8,128)(2,1)S(1)}, bf16[1024,512]{1,0:T(8,128)(2,1)}, u32[]{:S(2)}) copy-start(bf16[1024,512]{1,0:T(8,128)(2,1)} %param.17) | copy-start | bytes 3145732
  30.7 1.1 copy-start.7
  32.2 32.3 %collective-permute-start.4 = (bf16[64,1,512]{2,0,1:T(8,128)(2,1)S(1)}, bf16[64,1,512]{2,0,1:T(8,128)(2,1)S(1)}, u32[]{:S(2)}, u32[]{:S(2)}) collective-permute-start(bf16[64,1,512]{2,0,1:T(8,128)(2,1)S(1)} %get-tuple-element.29), channel_id=1, source_target_pairs={{0,64},{8,72},{16,80},{24,88},{32,96},{40,104},{48,112},{56,120},{... | collective-permute-start | bytes 196616 | tf_op jit(solution)/shard_map/ppermute | solution.py:22
  37.4 61.6 %collective-permute-start.10 = (bf16[64,1,512]{2,0,1:T(8,128)(2,1)S(1)}, bf16[64,1,512]{2,0,1:T(8,128)(2,1)S(1)}, u32[]{:S(2)}, u32[]{:S(2)}) collective-permute-start(bf16[64,1,512]{2,0,1:T(8,128)(2,1)S(1)} %get-tuple-element.23), channel_id=1, source_target_pairs={{0,448},{8,456},{16,464},{24,472},{32,480},{40,488},{48,496},{56,5... | collective-permute-start | bytes 196616 | tf_op jit(solution)/shard_map/ppermute | solution.py:22
  45.1 53.9 %collective-permute-start.9 = (bf16[64,1,512]{2,0,1:T(8,128)(2,1)S(1)}, bf16[64,1,512]{2,0,1:T(8,128)(2,1)S(1)}, u32[]{:S(2)}, u32[]{:S(2)}) collective-permute-start(bf16[64,1,512]{2,0,1:T(8,128)(2,1)S(1)} %get-tuple-element.24), channel_id=1, source_target_pairs={{0,384},{8,392},{16,400},{24,408},{32,416},{40,424},{48,432},{56,4... | collective-permute-start | bytes 196616 | tf_op jit(solution)/shard_map/ppermute | solution.py:22
  52.0 46.9 %collective-permute-start.8 = (bf16[64,1,512]{2,0,1:T(8,128)(2,1)S(1)}, bf16[64,1,512]{2,0,1:T(8,128)(2,1)S(1)}, u32[]{:S(2)}, u32[]{:S(2)}) collective-permute-start(bf16[64,1,512]{2,0,1:T(8,128)(2,1)S(1)} %get-tuple-element.25), channel_id=1, source_target_pairs={{0,320},{8,328},{16,336},{24,344},{32,352},{40,360},{48,368},{56,3... | collective-permute-start | bytes 196616 | tf_op jit(solution)/shard_map/ppermute | solution.py:22
  56.9 42.0 %collective-permute-start.7 = (bf16[64,1,512]{2,0,1:T(8,128)(2,1)S(1)}, bf16[64,1,512]{2,0,1:T(8,128)(2,1)S(1)}, u32[]{:S(2)}, u32[]{:S(2)}) collective-permute-start(bf16[64,1,512]{2,0,1:T(8,128)(2,1)S(1)} %get-tuple-element.26), channel_id=1, source_target_pairs={{0,256},{8,264},{16,272},{24,280},{32,288},{40,296},{48,304},{56,3... | collective-permute-start | bytes 196616 | tf_op jit(solution)/shard_map/ppermute | solution.py:22
  64.5 15.8 %collective-permute-start.5 = (bf16[64,1,512]{2,0,1:T(8,128)(2,1)S(1)}, bf16[64,1,512]{2,0,1:T(8,128)(2,1)S(1)}, u32[]{:S(2)}, u32[]{:S(2)}) collective-permute-start(bf16[64,1,512]{2,0,1:T(8,128)(2,1)S(1)} %get-tuple-element.28), channel_id=1, source_target_pairs={{0,128},{8,136},{16,144},{24,152},{32,160},{40,168},{48,176},{56,1... | collective-permute-start | bytes 196616 | tf_op jit(solution)/shard_map/ppermute | solution.py:22
  80.3 18.5 %collective-permute-start.6 = (bf16[64,1,512]{2,0,1:T(8,128)(2,1)S(1)}, bf16[64,1,512]{2,0,1:T(8,128)(2,1)S(1)}, u32[]{:S(2)}, u32[]{:S(2)}) collective-permute-start(bf16[64,1,512]{2,0,1:T(8,128)(2,1)S(1)} %get-tuple-element.27), channel_id=1, source_target_pairs={{0,192},{8,200},{16,208},{24,216},{32,224},{40,232},{48,240},{56,2... | collective-permute-start | bytes 196616 | tf_op jit(solution)/shard_map/ppermute | solution.py:22
  99.0 0.8 copy-start.3
  99.8 8.3 %copy-start.8 = (s32[64]{0:T(128)S(1)}, s32[64]{0:T(128)}, u32[]{:S(2)}) copy-start(s32[64]{0:T(128)} %get-tuple-element.44) | copy-start | bytes 772
  99.8 8.3 %copy-start.9 = (s32[64]{0:T(128)S(1)}, s32[64]{0:T(128)}, u32[]{:S(2)}) copy-start(s32[64]{0:T(128)} %get-tuple-element.45) | copy-start | bytes 772
  102.4 14.7 %all-to-all-start = ((bf16[8,8,1,8,1,512]{5,3,0,4,2,1:T(8,128)(2,1)}), bf16[8,8,1,8,1,512]{5,3,0,4,2,1:T(8,128)(2,1)S(1)}, u32[]{:S(2)}, u32[]{:S(2)}) async-start(bf16[8,8,1,8,1,512]{5,3,0,4,2,1:T(8,128)(2,1)} %copy.49), calls=%async_computation | async-start | bytes 1048576 | tf_op jit(solution)/shard_map/all_to_all | solution.py:159
  152.5 24.5 %collective-permute-start.11 = (bf16[64,1,512]{2,0,1:T(8,128)(2,1)S(1)}, bf16[64,1,512]{2,0,1:T(8,128)(2,1)S(1)}, u32[]{:S(2)}, u32[]{:S(2)}) collective-permute-start(bf16[64,1,512]{2,0,1:T(8,128)(2,1)S(1)} %get-tuple-element.21), channel_id=1, source_target_pairs={{0,64},{8,72},{16,80},{24,88},{32,96},{40,104},{48,112},{56,120},{... | collective-permute-start | bytes 196616 | tf_op jit(solution)/shard_map/ppermute | solution.py:22
  154.5 47.0 %collective-permute-start.17 = (bf16[64,1,512]{2,0,1:T(8,128)(2,1)S(1)}, bf16[64,1,512]{2,0,1:T(8,128)(2,1)S(1)}, u32[]{:S(2)}, u32[]{:S(2)}) collective-permute-start(bf16[64,1,512]{2,0,1:T(8,128)(2,1)S(1)} %get-tuple-element.15), channel_id=1, source_target_pairs={{0,448},{8,456},{16,464},{24,472},{32,480},{40,488},{48,496},{56,5... | collective-permute-start | bytes 196616 | tf_op jit(solution)/shard_map/ppermute | solution.py:22
  160.5 40.9 %collective-permute-start.16 = (bf16[64,1,512]{2,0,1:T(8,128)(2,1)S(1)}, bf16[64,1,512]{2,0,1:T(8,128)(2,1)S(1)}, u32[]{:S(2)}, u32[]{:S(2)}) collective-permute-start(bf16[64,1,512]{2,0,1:T(8,128)(2,1)S(1)} %get-tuple-element.16), channel_id=1, source_target_pairs={{0,384},{8,392},{16,400},{24,408},{32,416},{40,424},{48,432},{56,4... | collective-permute-start | bytes 196616 | tf_op jit(solution)/shard_map/ppermute | solution.py:22
  162.4 39.0 %collective-permute-start.15 = (bf16[64,1,512]{2,0,1:T(8,128)(2,1)S(1)}, bf16[64,1,512]{2,0,1:T(8,128)(2,1)S(1)}, u32[]{:S(2)}, u32[]{:S(2)}) collective-permute-start(bf16[64,1,512]{2,0,1:T(8,128)(2,1)S(1)} %get-tuple-element.17), channel_id=1, source_target_pairs={{0,320},{8,328},{16,336},{24,344},{32,352},{40,360},{48,368},{56,3... | collective-permute-start | bytes 196616 | tf_op jit(solution)/shard_map/ppermute | solution.py:22
  166.5 34.9 %collective-permute-start.14 = (bf16[64,1,512]{2,0,1:T(8,128)(2,1)S(1)}, bf16[64,1,512]{2,0,1:T(8,128)(2,1)S(1)}, u32[]{:S(2)}, u32[]{:S(2)}) collective-permute-start(bf16[64,1,512]{2,0,1:T(8,128)(2,1)S(1)} %get-tuple-element.18), channel_id=1, source_target_pairs={{0,256},{8,264},{16,272},{24,280},{32,288},{40,296},{48,304},{56,3... | collective-permute-start | bytes 196616 | tf_op jit(solution)/shard_map/ppermute | solution.py:22
  177.0 10.9 %collective-permute-start.12 = (bf16[64,1,512]{2,0,1:T(8,128)(2,1)S(1)}, bf16[64,1,512]{2,0,1:T(8,128)(2,1)S(1)}, u32[]{:S(2)}, u32[]{:S(2)}) collective-permute-start(bf16[64,1,512]{2,0,1:T(8,128)(2,1)S(1)} %get-tuple-element.20), channel_id=1, source_target_pairs={{0,128},{8,136},{16,144},{24,152},{32,160},{40,168},{48,176},{56,1... | collective-permute-start | bytes 196616 | tf_op jit(solution)/shard_map/ppermute | solution.py:22
  187.9 13.5 %collective-permute-start.13 = (bf16[64,1,512]{2,0,1:T(8,128)(2,1)S(1)}, bf16[64,1,512]{2,0,1:T(8,128)(2,1)S(1)}, u32[]{:S(2)}, u32[]{:S(2)}) collective-permute-start(bf16[64,1,512]{2,0,1:T(8,128)(2,1)S(1)} %get-tuple-element.19), channel_id=1, source_target_pairs={{0,192},{8,200},{16,208},{24,216},{32,224},{40,232},{48,240},{56,2... | collective-permute-start | bytes 196616 | tf_op jit(solution)/shard_map/ppermute | solution.py:22
  201.5 0.8 copy-start.2
where the time goes:
time: 208 us; the launch traced here: 206 us
  starting transfers between devices  90.2 us (43%)
  waiting for transfers between devices  55.3 us (27%)
  local copies, waits for them, and re-layouts  24.7 us (12%)
  matrix products  12.3 us (6%)
  blocking collectives  11.7 us (6%)
  other arithmetic  11.4 us (5%)
    ppermute x14, starting transfers between devices, passed_along(): lax.ppermute(x, axis, [(i, (i + by) % devices) for i in range(devices)])  70.6 us
    ppermute x14, waiting for transfers between devices, passed_along(): lax.ppermute(x, axis, [(i, (i + by) % devices) for i in range(devices)])  44.8 us
    all_to_all x1, blocking collectives, on_device(): lax.all_to_all(returning, 'cols', split_axis=2, concat_axis=1, tiled=True)  11.7 us
    ppermute x2, starting transfers between devices, extended(): after = lax.ppermute(first, axis, down)  8.43 us
    ppermute x2, waiting for transfers between devices, extended(): after = lax.ppermute(first, axis, down)  5.71 us
    all_to_all x1, starting transfers between devices, on_device(): lax.all_to_all(sectioned, 'cols', split_axis=1, concat_axis=2, tiled=True)  5.65 us
    ppermute x2, starting transfers between devices, extended(): before = lax.ppermute(last, axis, up)  5.51 us
    reshape x1, local copies, waits for them, and re-layouts, grid_attention(): projected.astype(jnp.bfloat16)  5.13 us
  transfers between devices with their start and end apart: 19, of which 9 were waited for; matrix products, arithmetic and copies ran while one was open for 3% of the time, Pallas kernels for 0%

commit v1 on v0

v1 whole, which is shorter than its diff:
```python
import jax
import jax.numpy as jnp
from jax import lax
from jax.experimental import pallas as pl
from jax.experimental.pallas import tpu as pltpu
from jax.sharding import PartitionSpec as P

MESH = pl.DeviceIdType.MESH
F32 = jnp.float32
BF16 = jnp.bfloat16

FORECASTS = 2
ROWS = 8
COLS = 32
CELLS = ROWS * COLS
WIDTH = 512
INNER = 1024
SIDE = 8
PEERS = SIDE * SIDE
PIECE = 16
GROUPS = CELLS // PEERS
PADDED = 40
QUADS = 4


def gelu(v):
    half = 0.5 * v
    return half + half * jnp.tanh(v * (0.7978845608028654 + 0.035677408136300125 * (v * v)))


def layer_norm(v, gain):
    centred = v - jnp.mean(v, axis=-1, keepdims=True)
    variance = jnp.mean(centred * centred, axis=-1, keepdims=True)
    return centred * lax.rsqrt(variance + 1e-05) * gain


def iota(shape, dim):
    return lax.broadcasted_iota(jnp.int32, shape, dim)


def one_hot(condition):
    return jnp.where(condition, 1.0, 0.0).astype(BF16)


def matmul(a, b):
    return jnp.dot(a, b, preferred_element_type=F32)


def kernel(
    x_hbm, premix_ref, we_hbm, dw_ref, db_ref, wp_hbm, gain_ref, wqkv_hbm, wo_hbm, table_ref,
    out_hbm,
    xb, we, wp, wqkv, wo, edge, halo_rows, halo_edge, normed, ex, act, conv, pk,
    snd, rcv, bsnd, brcv, xg, qkv, flat, shifted, bias, ob,
    load_sem, halo_send, halo_recv, own_sem, fwd_send, fwd_recv, back_send, back_recv, out_sem,
):
    r = lax.axis_index("rows")
    c = lax.axis_index("cols")
    n_rows = lax.axis_size("rows")
    n_cols = lax.axis_size("cols")
    a, m = r // SIDE, r % SIDE
    me = a * SIDE + c

    loads = [
        pltpu.make_async_copy(src, dst, load_sem.at[i])
        for i, (src, dst) in enumerate(
            ((x_hbm, xb), (we_hbm, we), (wp_hbm, wp), (wqkv_hbm, wqkv), (wo_hbm, wo))
        )
    ]
    for load in loads:
        load.start()

    north, south = lax.rem(r + n_rows - 1, n_rows), lax.rem(r + 1, n_rows)
    west, east = lax.rem(c + n_cols - 1, n_cols), lax.rem(c + 1, n_cols)

    def peer(k):
        return lax.rem(a + k % SIDE, SIDE), lax.rem(c + k // SIDE, SIDE)

    barrier = pltpu.get_barrier_semaphore()
    for row, col in (
        (north, c), (south, c), (north, west), (north, east), (south, west), (south, east),
    ):
        pl.semaphore_signal(barrier, inc=1, device_id=(row, col), device_id_type=MESH)

    def greet(k, carry):
        pa, pc = peer(k)
        pl.semaphore_signal(barrier, inc=1, device_id=(pa * SIDE + m, pc), device_id_type=MESH)
        return carry

    lax.fori_loop(1, PEERS, greet, 0)

    loads[0].wait()
    place = iota((96, 512), 0)
    piece, index = place // 16, place % 16
    cell_f = jnp.where(piece < 2, index // 8, index % 2)
    cell_y = jnp.where(piece < 2, index % 8, jnp.where(piece < 4, 0, 7))
    cell_x = jnp.where(piece % 2 == 0, 0, 31)
    chosen = iota((96, 512), 1) == cell_f * CELLS + cell_y * COLS + cell_x
    edge[...] = matmul(one_hot(chosen), xb[...].reshape(512, WIDTH)).astype(BF16).reshape(6, 16, WIDTH)

    pl.semaphore_wait(barrier, PEERS - 1 + 6)

    def halo(i, src, dst, row, col):
        return pltpu.make_async_remote_copy(
            src_ref=src,
            dst_ref=dst,
            send_sem=halo_send.at[i],
            recv_sem=halo_recv.at[i],
            device_id=(row, col),
            device_id_type=MESH,
        )

    halos = [
        halo(0, xb.at[:, ROWS - 1], halo_rows.at[0], south, c),
        halo(1, xb.at[:, 0], halo_rows.at[1], north, c),
        halo(2, edge.at[0], halo_edge.at[0], r, west),
        halo(3, edge.at[1], halo_edge.at[1], r, east),
        halo(4, edge.at[5], halo_edge.at[2], south, east),
        halo(5, edge.at[4], halo_edge.at[3], south, west),
        halo(6, edge.at[3], halo_edge.at[4], north, east),
        halo(7, edge.at[2], halo_edge.at[5], north, west),
    ]
    for copy in halos:
        copy.start()

    def forward(f, k):
        pa, pc = peer(k)
        o = pa * SIDE + pc
        return pltpu.make_async_remote_copy(
            src_ref=snd.at[f, pl.ds(pl.multiple_of(o * PIECE, PIECE), PIECE)],
            dst_ref=rcv.at[f, pl.ds(pl.multiple_of(me * PIECE, PIECE), PIECE)],
            send_sem=fwd_send.at[f],
            recv_sem=fwd_recv.at[f],
            device_id=(pa * SIDE + m, pc),
            device_id_type=MESH,
        )

    def backward(f, k):
        pa, pc = peer(k)
        o = pa * SIDE + pc
        return pltpu.make_async_remote_copy(
            src_ref=bsnd.at[f, pl.ds(pl.multiple_of(o * PIECE, PIECE), PIECE)],
            dst_ref=brcv.at[f, pl.ds(pl.multiple_of(me * PIECE, PIECE), PIECE)],
            send_sem=back_send.at[f],
            recv_sem=back_recv.at[f],
            device_id=(pa * SIDE + m, pc),
            device_id_type=MESH,
        )

    def own(f, src, dst):
        mine = pl.ds(pl.multiple_of(me * PIECE, PIECE), PIECE)
        return pltpu.make_async_copy(src.at[f, mine], dst.at[f, mine], own_sem)

    def wait_all(f, ref, sem):
        others = ref.at[f, pl.ds(0, (PEERS - 1) * PIECE)]
        pltpu.make_async_copy(others, others, sem.at[f]).wait()

    premix = premix_ref[...]
    gain = gain_ref[...]

    def convolve(f, carry):
        def norm_rows(i, carry):
            v = xb[f, pl.ds(2 * i, 2)].astype(F32).reshape(64, WIDTH)
            normed[pl.ds(pl.multiple_of(i * 64, 64), 64)] = layer_norm(v, premix).astype(BF16)
            return carry

        lax.fori_loop(0, 4, norm_rows, 0)

        @pl.when(f == 0)
        def _():
            loads[1].wait()

        def expand_tile(i, carry):
            lanes = pl.ds(pl.multiple_of(i * 256, 256), 256)
            g = gelu(matmul(normed[0:CELLS], we[:, lanes])).astype(BF16).astype(F32)
            ex[1 : ROWS + 1, 0:COLS, lanes] = g.reshape(ROWS, COLS, 256)
            return carry

        lax.fori_loop(0, INNER // 256, expand_tile, 0)

        @pl.when(f == 0)
        def _():
            for copy in halos:
                copy.wait_recv()

        top = halo_rows[0, f].astype(F32) * jnp.where(r == 0, 0.0, 1.0)
        bottom = halo_rows[1, f].astype(F32) * jnp.where(r == n_rows - 1, 0.0, 1.0)
        normed[256:288] = layer_norm(top, premix).astype(BF16)
        normed[288:320] = layer_norm(bottom, premix).astype(BF16)
        place = iota((80, 96), 0)
        y, slot = place // 8, place % 8
        inside = ((y > 0) | (r > 0)) & ((y < 9) | (r < n_rows - 1))
        in_east = (slot == 0) & (c < n_cols - 1)
        in_west = (slot == 7) & (c > 0)
        source_east = jnp.where(y == 0, 48 + f, jnp.where(y == 9, 80 + f, f * 8 + y - 1))
        source_west = jnp.where(y == 0, 32 + f, jnp.where(y == 9, 64 + f, 16 + f * 8 + y - 1))
        source = jnp.where(in_east, source_east, source_west)
        chosen = (iota((80, 96), 1) == source) & inside & (in_east | in_west)
        sides = matmul(one_hot(chosen), halo_edge[...].reshape(96, WIDTH))
        normed[320:400] = layer_norm(sides, premix).astype(BF16)

        def expand_halo(i, carry):
            lanes = pl.ds(pl.multiple_of(i * 256, 256), 256)
            g = gelu(matmul(normed[CELLS:400], we[:, lanes])).astype(BF16).astype(F32)
            ex[0, 0:COLS, lanes] = g[0:32]
            ex[ROWS + 1, 0:COLS, lanes] = g[32:64]
            ex[:, COLS:PADDED, lanes] = g[64:144].reshape(ROWS + 2, 8, 256)
            return carry

        lax.fori_loop(0, INNER // 256, expand_halo, 0)

        def filter_row(y, carry):
            for i in range(INNER // 256):
                lanes = slice(i * 256, (i + 1) * 256)
                around = [ex[y + q, :, lanes] for q in range(3)]
                taps = [
                    sum(around[q] * dw_ref[q, s : s + 1, lanes] for q in range(3)) for s in range(3)
                ]
                total = (
                    pltpu.roll(taps[0], 1, 0) + taps[1] + pltpu.roll(taps[2], PADDED - 1, 0)
                )
                act[pl.ds(pl.multiple_of(y * COLS, COLS), COLS), lanes] = gelu(
                    total[0:COLS] + db_ref[:, lanes]
                ).astype(BF16)
            return carry

        lax.fori_loop(0, ROWS, filter_row, 0)

        @pl.when(f == 0)
        def _():
            loads[2].wait()

        for i in range(2):
            lanes = slice(i * 256, (i + 1) * 256)
            residual = xb[f, :, :, lanes].astype(F32).reshape(CELLS, 256)
            conv[f, :, lanes] = (residual + matmul(act[...], wp[:, lanes])).astype(BF16)

        def norm_out(i, carry):
            rows = pl.ds(pl.multiple_of(i * 64, 64), 64)
            v = layer_norm(conv[f, rows].astype(F32), gain)
            for q in range(4):
                pk[pl.ds(i * 256 + q, 64, stride=4), :] = v[:, q * 128 : (q + 1) * 128]
            return carry

        lax.fori_loop(0, 4, norm_out, 0)
        snd[f] = pk[...].astype(BF16)

        def send(k, carry):
            forward(f, k).start()
            return carry

        lax.fori_loop(1, PEERS, send, 0)
        copy = own(f, snd, rcv)
        copy.start()
        copy.wait()
        return carry

    lax.fori_loop(0, FORECASTS, convolve, 0)

    flat[...] = jnp.zeros_like(flat)
    total = jnp.zeros((16, 256), F32)
    for q in range(15):
        flat[:, 0:15] = table_ref[:, q, :]
        total = total + (pltpu.roll(flat[...], 16 * q, 1) if q else flat[...])
    flat[...] = total

    def shift(j, carry):
        moved = pltpu.roll(flat[...], 137 + 16 * (j // 8) + j % 8, 1)
        shifted[:, pl.ds(j, 1), :] = moved[:, 0:128].reshape(16, 1, 128)
        return carry

    lax.fori_loop(0, PEERS, shift, 0)
    source, target = iota((512, 256), 0), iota((512, 256), 1)
    member = target % 64
    spread = one_hot(source == (target // 64) * 128 + 16 * (member // 8) + member % 8)

    def set_bias(q, carry):
        rest = jnp.concatenate([shifted[q * 4 + h] for h in range(4)], axis=1)
        total = jnp.zeros((64, 256), F32)
        for _ in range(3):
            part = rest.astype(BF16)
            total = total + matmul(part, spread)
            rest = rest - part.astype(F32)
        bias[q] = total
        return carry

    lax.fori_loop(0, QUADS, set_bias, 0)
    loads[3].wait()

    head = iota((1, 128), 1) // 32
    own_lanes = [head == h for h in range(4)]

    def attend(f, carry):
        wait_all(f, rcv, fwd_recv)
        pk[...] = rcv[f].astype(F32)
        for t in range(GROUPS):
            for q in range(4):
                xg[t * 64 : (t + 1) * 64, q * 128 : (q + 1) * 128] = pk[
                    pl.ds(t * 4 + q, 64, stride=PIECE), :
                ].astype(BF16)

        def project(i, carry):
            lanes = pl.ds(pl.multiple_of(i * 256, 256), 256)
            qkv[:, lanes] = matmul(xg[...], wqkv[:, lanes]).astype(BF16)
            return carry

        lax.fori_loop(0, 6, project, 0)

        def group(t, carry):
            rows = pl.ds(pl.multiple_of(t * 64, 64), 64)
            for q in range(QUADS):
                lanes = slice(q * 128, (q + 1) * 128)
                query = qkv[rows, lanes]
                keys = qkv[rows, 512 + q * 128 : 640 + q * 128]
                values = qkv[rows, 1024 + q * 128 : 1152 + q * 128]
                apart = jnp.concatenate(
                    [query * one_hot(own_lanes[h]) for h in range(4)], axis=0
                )
                scores = lax.dot_general(
                    keys, apart, (((1,), (1,)), ((), ())), preferred_element_type=F32
                )
                scores = scores * (32**-0.5) + bias[q]
                powers = jnp.exp(scores - jnp.max(scores, axis=0, keepdims=True))
                share = 1.0 / jnp.sum(powers, axis=0, keepdims=True)
                attention = (powers * share).astype(BF16)
                mixed = lax.dot_general(
                    attention, values, (((0,), (0,)), ((), ())), preferred_element_type=F32
                )
                context = jnp.where(own_lanes[0], mixed[0:64], 0.0)
                for h in range(1, 4):
                    context = jnp.where(own_lanes[h], mixed[h * 64 : (h + 1) * 64], context)
                pk[pl.ds(t * 4 + q, 64, stride=PIECE), :] = context
            return carry

        lax.fori_loop(0, GROUPS, group, 0)
        bsnd[f] = pk[...].astype(BF16)

        def send(k, carry):
            backward(f, k).start()
            return carry

        lax.fori_loop(1, PEERS, send, 0)
        copy = own(f, bsnd, brcv)
        copy.start()
        copy.wait()
        return carry

    lax.fori_loop(0, FORECASTS, attend, 0)
    loads[4].wait()

    def finish(f, carry):
        wait_all(f, brcv, back_recv)
        pk[...] = brcv[f].astype(F32)
        for q in range(4):
            xg[:, q * 128 : (q + 1) * 128] = pk[pl.ds(q, CELLS, stride=4), :].astype(BF16)
        for i in range(2):
            lanes = slice(i * 256, (i + 1) * 256)
            total = conv[f, :, lanes].astype(F32) + matmul(xg[...], wo[:, lanes])
            ob[f, :, :, lanes] = total.astype(BF16).reshape(ROWS, COLS, 256)
        pltpu.make_async_copy(ob.at[f], out_hbm.at[f], out_sem.at[f]).start()
        return carry

    lax.fori_loop(0, FORECASTS, finish, 0)

    for copy in halos:
        copy.wait_send()
    for f in range(FORECASTS):
        wait_all(f, snd, fwd_send)
        wait_all(f, bsnd, back_send)
        pltpu.make_async_copy(ob.at[f], out_hbm.at[f], out_sem.at[f]).wait()


def on_device(
    atmosphere_variables,
    premix_gain_vector,
    expand_weight,
    depth_weight,
    depth_bias,
    project_weight,
    norm_attn,
    qkv_weight,
    out_weight,
    bias_table,
):
    whole = pl.BlockSpec(memory_space=pl.ANY)
    small = pl.BlockSpec(memory_space=pltpu.VMEM)
    tile = (FORECASTS, ROWS, COLS, WIDTH)
    pieces = (FORECASTS, PEERS * PIECE, 128)
    return pl.pallas_call(
        kernel,
        out_shape=jax.ShapeDtypeStruct(tile, BF16),
        in_specs=[whole, small, whole, small, small, whole, small, whole, whole, small],
        out_specs=whole,
        scratch_shapes=[
            pltpu.VMEM(tile, BF16),
            pltpu.VMEM((WIDTH, INNER), BF16),
            pltpu.VMEM((INNER, WIDTH), BF16),
            pltpu.VMEM((WIDTH, 3 * WIDTH), BF16),
            pltpu.VMEM((WIDTH, WIDTH), BF16),
            pltpu.VMEM((6, 16, WIDTH), BF16),
            pltpu.VMEM((2, FORECASTS, COLS, WIDTH), BF16),
            pltpu.VMEM((6, 16, WIDTH), BF16),
            pltpu.VMEM((400, WIDTH), BF16),
            pltpu.VMEM((ROWS + 2, PADDED, INNER), F32),
            pltpu.VMEM((CELLS, INNER), BF16),
            pltpu.VMEM((FORECASTS, CELLS, WIDTH), BF16),
            pltpu.VMEM((PEERS * PIECE, 128), F32),
            pltpu.VMEM(pieces, BF16),
            pltpu.VMEM(pieces, BF16),
            pltpu.VMEM(pieces, BF16),
            pltpu.VMEM(pieces, BF16),
            pltpu.VMEM((CELLS, WIDTH), BF16),
            pltpu.VMEM((CELLS, 3 * WIDTH), BF16),
            pltpu.VMEM((16, 256), F32),
            pltpu.VMEM((16, PEERS, 128), F32),
            pltpu.VMEM((QUADS, 64, 256), F32),
            pltpu.VMEM(tile, BF16),
            pltpu.SemaphoreType.DMA((5,)),
            pltpu.SemaphoreType.DMA((8,)),
            pltpu.SemaphoreType.DMA((8,)),
            pltpu.SemaphoreType.DMA,
            pltpu.SemaphoreType.DMA((FORECASTS,)),
            pltpu.SemaphoreType.DMA((FORECASTS,)),
            pltpu.SemaphoreType.DMA((FORECASTS,)),
            pltpu.SemaphoreType.DMA((FORECASTS,)),
            pltpu.SemaphoreType.DMA((FORECASTS,)),
        ],
        compiler_params=pltpu.CompilerParams(
            collective_id=0, has_side_effects=True, vmem_limit_bytes=40 * 1024 * 1024
        ),
        name="maxvit_layer",
    )(
        atmosphere_variables,
        premix_gain_vector.reshape(1, WIDTH),
        expand_weight,
        depth_weight,
        depth_bias.reshape(1, INNER),
        project_weight,
        norm_attn.reshape(1, WIDTH),
        qkv_weight,
        out_weight,
        bias_table,
    )


def solution(mesh):
    return jax.shard_map(
        on_device,
        mesh=mesh,
        in_specs=(P(None, "rows", "cols", None), P(), P(), P(), P(), P(), P(), P(), P(), P()),
        out_specs=P(None, "rows", "cols", None),
        check_vma=False,
    )
```

time: 208 us -> 92.1 us (0.44)
  the two profiles are of different devices: /device:TPU:34 before, /device:TPU:1 now
where the time goes in v1:
time: 92.1 us; the launch traced here: 91.7 us
  Pallas kernels  81.1 us (88%)
  local copies, waits for them, and re-layouts  10.5 us (11%)
    pallas_call x1, Pallas kernels, on_device(): pl.pallas_call(kernel, out_shape=jax.ShapeDtypeStruct(tile, BF16), in_spe...  81.1 us
    unnamed x20, local copies, waits for them, and re-layouts  10.5 us

profile of v1, /device:TPU:1, one launch (start us, length us, event | category | flops | bytes accessed | tf_op | source)
XLA Modules:
  0.0 91.7 jit_solution(8059643792953346721)
XLA Ops:
  0.0 0.9 %copy.11.table_ref = f32[16,15,15]{2,1,0:T(8,128)S(1)} copy(f32[16,15,15]{2,0,1:T(8,128)} %param.19) | data formatting | bytes 28800 | tf_op args[9]
  0.9 0.0 copy-start
  1.0 1.4 %copy-done = bf16[512,1536]{1,0:T(8,128)(2,1)S(1)} copy-done((bf16[512,1536]{1,0:T(8,128)(2,1)S(1)}, bf16[512,1536]{1,0:T(8,128)(2,1)}, u32[]{:S(2)}) %copy-start) | copy-done | bytes 1572888
  2.4 0.0 copy-start.1
  2.4 1.2 %copy-done.1 = bf16[512,1024]{1,0:T(8,128)(2,1)S(1)} copy-done((bf16[512,1024]{1,0:T(8,128)(2,1)S(1)}, bf16[512,1024]{1,0:T(8,128)(2,1)}, u32[]{:S(2)}) %copy-start.1) | copy-done | bytes 1048600
  3.6 0.0 copy-start.2
  3.6 1.2 %copy-done.2 = bf16[1024,512]{1,0:T(8,128)(2,1)S(1)} copy-done((bf16[1024,512]{1,0:T(8,128)(2,1)S(1)}, bf16[1024,512]{1,0:T(8,128)(2,1)}, u32[]{:S(2)}) %copy-start.2) | copy-done | bytes 1048600
  4.8 0.0 copy-start.3
  4.8 1.0 %copy-done.3 = bf16[2,8,32,512]{3,2,1,0:T(8,128)(2,1)S(1)} copy-done((bf16[2,8,32,512]{3,2,1,0:T(8,128)(2,1)S(1)}, bf16[2,8,32,512]{3,2,1,0:T(8,128)(2,1)}, u32[]{:S(2)}) %copy-start.3) | copy-done | bytes 524312
  5.9 0.0 copy-start.4
  5.9 1.0 %copy-done.4 = bf16[512,512]{1,0:T(8,128)(2,1)S(1)} copy-done((bf16[512,512]{1,0:T(8,128)(2,1)S(1)}, bf16[512,512]{1,0:T(8,128)(2,1)}, u32[]{:S(2)}) %copy-start.4) | copy-done | bytes 524312
  6.9 0.0 copy-start.5
  6.9 0.8 copy-done.5
  7.7 0.0 copy-start.6
  7.7 0.7 copy-done.6
  8.4 0.0 copy-start.7
  8.4 0.7 copy-done.7
  9.1 0.0 copy-start.8
  9.1 0.7 copy-done.8
  9.7 81.1 %maxvit_layer.1 = bf16[2,8,32,512]{3,2,1,0:T(8,128)(2,1)S(1)} custom-call(bf16[2,8,32,512]{3,2,1,0:T(8,128)(2,1)S(1)} %copy-done.3, f32[1,512]{1,0:T(1,128)S(1)} %bitcast.4, bf16[512,1024]{1,0:T(8,128)(2,1)S(1)} %copy-done.1, f32[3,3,1024]{2,1,0:T(4,128)S(1)} %copy-done.5, f32[1,1024]{1,0:T(1,128)S(1)} %bitcast.3, bf16[1024,512]{1,0:T(8,128)(2,1)S(1)} %copy-done.2, ...), custom_call_target="tpu_custom_call" | custom-call | tf_op jit(solution)/shard_map/maxvit_layer/pallas_call | solution.py:388
  90.9 0.8 copy.13
Async XLA Ops:
  0.9 1.4 %copy-start = (bf16[512,1536]{1,0:T(8,128)(2,1)S(1)}, bf16[512,1536]{1,0:T(8,128)(2,1)}, u32[]{:S(2)}) copy-start(bf16[512,1536]{1,0:T(8,128)(2,1)} %wqkv_hbm.1) | copy-start | bytes 4718596
  2.4 1.2 %copy-start.1 = (bf16[512,1024]{1,0:T(8,128)(2,1)S(1)}, bf16[512,1024]{1,0:T(8,128)(2,1)}, u32[]{:S(2)}) copy-start(bf16[512,1024]{1,0:T(8,128)(2,1)} %we_hbm.1) | copy-start | bytes 3145732
  3.6 1.2 %copy-start.2 = (bf16[1024,512]{1,0:T(8,128)(2,1)S(1)}, bf16[1024,512]{1,0:T(8,128)(2,1)}, u32[]{:S(2)}) copy-start(bf16[1024,512]{1,0:T(8,128)(2,1)} %wp_hbm.1) | copy-start | bytes 3145732
  4.8 1.0 %copy-start.3 = (bf16[2,8,32,512]{3,2,1,0:T(8,128)(2,1)S(1)}, bf16[2,8,32,512]{3,2,1,0:T(8,128)(2,1)}, u32[]{:S(2)}) copy-start(bf16[2,8,32,512]{3,2,1,0:T(8,128)(2,1)} %x_hbm.1) | copy-start | bytes 1572868
  5.9 1.0 %copy-start.4 = (bf16[512,512]{1,0:T(8,128)(2,1)S(1)}, bf16[512,512]{1,0:T(8,128)(2,1)}, u32[]{:S(2)}) copy-start(bf16[512,512]{1,0:T(8,128)(2,1)} %wo_hbm.1) | copy-start | bytes 1572868
  6.9 0.8 copy-start.5
  7.7 0.7 copy-start.6
  8.4 0.7 copy-start.7
  9.1 0.7 copy-start.8

commit v2 on v1

v2 whole, which is shorter than its diff:
```python
import jax
import jax.numpy as jnp
from jax import lax
from jax.experimental import pallas as pl
from jax.experimental.pallas import tpu as pltpu
from jax.sharding import PartitionSpec as P

MESH = pl.DeviceIdType.MESH
F32 = jnp.float32
BF16 = jnp.bfloat16

FORECASTS = 2
ROWS = 8
COLS = 32
CELLS = ROWS * COLS
WIDTH = 512
INNER = 1024
SIDE = 8
PARTS = 4
PART_ROWS = FORECASTS * ROWS // PARTS
PART = PART_ROWS * COLS
PIECE = PART // SIDE
GROUPS = PIECE // SIDE
MEMBERS = SIDE * SIDE
PADDED = 40
QUADS = 4
LOG2E = 1.4426950408889634


def gelu(v):
    half = 0.5 * v
    return half + half * jnp.tanh(v * (0.7978845608028654 + 0.035677408136300125 * (v * v)))


def layer_norm(v, gain):
    centred = v - jnp.mean(v, axis=-1, keepdims=True)
    variance = jnp.mean(centred * centred, axis=-1, keepdims=True)
    return centred * lax.rsqrt(variance + 1e-05) * gain


def iota(shape, dim):
    return lax.broadcasted_iota(jnp.int32, shape, dim)


def one_hot(condition):
    return jnp.where(condition, 1.0, 0.0).astype(BF16)


def matmul(a, b):
    return jnp.dot(a, b, preferred_element_type=F32)


def kernel(
    x_hbm, premix_hbm, we_hbm, dw_hbm, db_hbm, wp_hbm, gain_hbm, wqkv_hbm, wo_hbm, table_hbm,
    out_hbm,
    xb, premix_ref, we, dw_ref, db_ref, wp, gain_ref, wqkv, wo, table_ref,
    edge, halo_rows, halo_edge, normed, ex, act, conv,
    att, mid, mid_out, owned, answers, mid_back, mid_return, returned,
    orders, xg, qkv, context, flat, shifted, bias, ob,
    load_sem, halo_send, halo_recv, sent, received, out_sem,
):
    r = lax.axis_index("rows")
    c = lax.axis_index("cols")
    n_rows = lax.axis_size("rows")
    n_cols = lax.axis_size("cols")
    a, m = r // SIDE, r % SIDE

    loads = [
        pltpu.make_async_copy(src, dst, load_sem.at[i])
        for i, (src, dst) in enumerate(
            (
                (x_hbm, xb), (premix_hbm, premix_ref), (we_hbm, we), (dw_hbm, dw_ref),
                (db_hbm, db_ref), (wp_hbm, wp), (gain_hbm, gain_ref), (table_hbm, table_ref),
                (wqkv_hbm, wqkv), (wo_hbm, wo),
            )
        )
    ]
    for load in loads[:3]:
        load.start()

    north, south = lax.rem(r + n_rows - 1, n_rows), lax.rem(r + 1, n_rows)
    west, east = lax.rem(c + n_cols - 1, n_cols), lax.rem(c + 1, n_cols)

    def along_rows(k):
        other = lax.rem(a + k, SIDE)
        return other, (other * SIDE + m, c)

    def along_cols(k):
        other = lax.rem(c + k, SIDE)
        return other, (r, other)

    barrier = pltpu.get_barrier_semaphore()
    for place in (
        (north, c), (south, c), (north, west), (north, east), (south, west), (south, east),
    ):
        pl.semaphore_signal(barrier, inc=1, device_id=place, device_id_type=MESH)

    def greet(k, carry):
        for along in (along_cols, along_rows):
            pl.semaphore_signal(barrier, inc=1, device_id=along(k)[1], device_id_type=MESH)
        return carry

    lax.fori_loop(1, SIDE, greet, 0)

    loads[0].wait()
    for load in loads[3:]:
        load.start()
    place = iota((96, 512), 0)
    piece, index = place // 16, place % 16
    cell_f = jnp.where(piece < 2, index // 8, index % 2)
    cell_y = jnp.where(piece < 2, index % 8, jnp.where(piece < 4, 0, 7))
    cell_x = jnp.where(piece % 2 == 0, 0, 31)
    chosen = iota((96, 512), 1) == cell_f * CELLS + cell_y * COLS + cell_x
    edge[...] = matmul(one_hot(chosen), xb[...].reshape(512, WIDTH)).astype(BF16).reshape(6, 16, WIDTH)

    pl.semaphore_wait(barrier, 2 * (SIDE - 1) + 6)

    def halo(i, src, dst, row, col):
        return pltpu.make_async_remote_copy(
            src_ref=src,
            dst_ref=dst,
            send_sem=halo_send.at[i],
            recv_sem=halo_recv.at[i],
            device_id=(row, col),
            device_id_type=MESH,
        )

    halos = [
        halo(0, xb.at[:, ROWS - 1], halo_rows.at[0], south, c),
        halo(1, xb.at[:, 0], halo_rows.at[1], north, c),
        halo(2, edge.at[0], halo_edge.at[0], r, west),
        halo(3, edge.at[1], halo_edge.at[1], r, east),
        halo(4, edge.at[5], halo_edge.at[2], south, east),
        halo(5, edge.at[4], halo_edge.at[3], south, west),
        halo(6, edge.at[3], halo_edge.at[4], north, east),
        halo(7, edge.at[2], halo_edge.at[5], north, west),
    ]
    for copy in halos:
        copy.start()

    def block(k):
        return pl.ds(pl.multiple_of(k * PIECE, PIECE), PIECE)

    def exchange(stage, p, src, dst, along, mine):
        def send(k, carry):
            other, place = along(k)
            pltpu.make_async_remote_copy(
                src_ref=src.at[p, block(other)],
                dst_ref=dst.at[p, block(mine)],
                send_sem=sent.at[stage, p],
                recv_sem=received.at[stage, p],
                device_id=place,
                device_id_type=MESH,
            ).start()
            return carry

        lax.fori_loop(1, SIDE, send, 0)
        dst[p, block(mine)] = src[p, block(mine)]

    def wait_all(ref, p, sem):
        others = ref.at[p, pl.ds(0, PART - PIECE)]
        pltpu.make_async_copy(others, others, sem).wait()

    loads[1].wait()
    premix = premix_ref[...]
    loads[2].wait()

    def expand_tile(f, carry):
        def norm_rows(i, carry):
            v = xb[f, pl.ds(2 * i, 2)].astype(F32).reshape(64, WIDTH)
            normed[pl.ds(pl.multiple_of(i * 64, 64), 64)] = layer_norm(v, premix).astype(BF16)
            return carry

        lax.fori_loop(0, 4, norm_rows, 0)

        def expand(i, carry):
            lanes = pl.ds(pl.multiple_of(i * 256, 256), 256)
            g = gelu(matmul(normed[0:CELLS], we[:, lanes])).astype(BF16).astype(F32)
            ex[f, 1 : ROWS + 1, 0:COLS, lanes] = g.reshape(ROWS, COLS, 256)
            return carry

        lax.fori_loop(0, INNER // 256, expand, 0)
        return carry

    lax.fori_loop(0, FORECASTS, expand_tile, 0)

    for copy in halos:
        copy.wait_recv()
    for load in loads[3:7]:
        load.wait()
    gain = gain_ref[...]

    def expand_halo(f):
        top = halo_rows[0, f].astype(F32) * jnp.where(r == 0, 0.0, 1.0)
        bottom = halo_rows[1, f].astype(F32) * jnp.where(r == n_rows - 1, 0.0, 1.0)
        normed[0:32] = layer_norm(top, premix).astype(BF16)
        normed[32:64] = layer_norm(bottom, premix).astype(BF16)
        place = iota((80, 96), 0)
        y, slot = place // 8, place % 8
        inside = ((y > 0) | (r > 0)) & ((y < 9) | (r < n_rows - 1))
        in_east = (slot == 0) & (c < n_cols - 1)
        in_west = (slot == 7) & (c > 0)
        source_east = jnp.where(y == 0, 48 + f, jnp.where(y == 9, 80 + f, f * 8 + y - 1))
        source_west = jnp.where(y == 0, 32 + f, jnp.where(y == 9, 64 + f, 16 + f * 8 + y - 1))
        source = jnp.where(in_east, source_east, source_west)
        chosen = (iota((80, 96), 1) == source) & inside & (in_east | in_west)
        sides = matmul(one_hot(chosen), halo_edge[...].reshape(96, WIDTH))
        normed[64:144] = layer_norm(sides, premix).astype(BF16)

        def expand(i, carry):
            lanes = pl.ds(pl.multiple_of(i * 256, 256), 256)
            g = gelu(matmul(normed[0:144], we[:, lanes])).astype(BF16).astype(F32)
            ex[f, 0, 0:COLS, lanes] = g[0:32]
            ex[f, ROWS + 1, 0:COLS, lanes] = g[32:64]
            ex[f, :, COLS:PADDED, lanes] = g[64:144].reshape(ROWS + 2, 8, 256)
            return carry

        lax.fori_loop(0, INNER // 256, expand, 0)

    def convolve(p, carry):
        f, first = p // 2, (p % 2) * PART_ROWS

        @pl.when(p % 2 == 0)
        def _():
            expand_halo(f)

        def filter_row(y, carry):
            for i in range(INNER // 256):
                lanes = slice(i * 256, (i + 1) * 256)
                around = [ex[f, first + y + q, :, lanes] for q in range(3)]
                taps = [
                    sum(around[q] * dw_ref[q, s : s + 1, lanes] for q in range(3)) for s in range(3)
                ]
                total = pltpu.roll(taps[0], 1, 0) + taps[1] + pltpu.roll(taps[2], PADDED - 1, 0)
                act[pl.ds(pl.multiple_of(y * COLS, COLS), COLS), lanes] = gelu(
                    total[0:COLS] + db_ref[:, lanes]
                ).astype(BF16)
            return carry

        lax.fori_loop(0, PART_ROWS, filter_row, 0)
        for i in range(2):
            lanes = slice(i * 256, (i + 1) * 256)
            residual = xb[f, pl.ds(first, PART_ROWS), :, lanes].astype(F32).reshape(PART, 256)
            conv[p, :, lanes] = (residual + matmul(act[...], wp[:, lanes])).astype(BF16)
        for i in range(2):
            rows = slice(i * 64, (i + 1) * 64)
            att[p, rows] = layer_norm(conv[p, rows].astype(F32), gain).astype(BF16)
        exchange(0, p, att, mid, along_rows, a)
        return carry

    lax.fori_loop(0, PARTS, convolve, 0)

    row, col = iota((PART, PART), 0), iota((PART, PART), 1)
    swapped = row // 16 * 2 + row % 16 // 2 * 16 + row % 2
    orders[0] = one_hot(col == swapped)
    grouped = row % 8 * 16 + row % 64 // 8 * 2 + row // 64
    orders[1] = one_hot(col == grouped)
    ungrouped = row % 2 * 64 + row % 16 // 2 * 8 + row // 16
    orders[2] = one_hot(col == ungrouped)

    def reorder(i, v):
        return matmul(orders[i], v).astype(BF16)

    def pass_on(p):
        wait_all(mid, p, received.at[0, p])
        mid_out[p] = reorder(0, mid[p])
        exchange(1, p, mid_out, owned, along_cols, c)

    pass_on(0)

    loads[7].wait()
    flat[...] = jnp.zeros_like(flat)
    total = jnp.zeros((16, 256), F32)
    for q in range(15):
        flat[:, 0:15] = table_ref[q]
        total = total + (pltpu.roll(flat[...], 16 * q, 1) if q else flat[...])
    flat[...] = total

    def shift(h, carry):
        row = jnp.broadcast_to(flat[pl.ds(h, 1), :], (8, 256))
        for i in range(SIDE):
            moved = pltpu.roll(row, 137 + 16 * i, 1, stride=1, stride_axis=0)
            shifted[h, i * 8 : (i + 1) * 8] = moved[:, 0:128]
        return carry

    lax.fori_loop(0, 16, shift, 0)
    source, target = iota((512, 256), 0), iota((512, 256), 1)
    member = target % 64
    spread = one_hot(source == (target // 64) * 128 + 16 * (member // 8) + member % 8)

    def set_bias(q, carry):
        rest = jnp.concatenate([shifted[q * 4 + h] for h in range(4)], axis=1)
        parts = []
        for _ in range(3):
            parts.append(rest.astype(BF16))
            rest = rest - parts[-1].astype(F32)
        total = matmul(jnp.concatenate(parts, axis=0), spread)
        bias[q] = (total[0:64] + total[64:128] + total[128:192]) * LOG2E
        return carry

    lax.fori_loop(0, QUADS, set_bias, 0)
    loads[8].wait()

    head = iota((1, 128), 1) // 32
    own_lanes = [head == h for h in range(4)]

    def attend(p, carry):
        wait_all(owned, p, received.at[1, p])
        xg[...] = reorder(1, owned[p])

        def project(i, carry):
            lanes = pl.ds(pl.multiple_of(i * 256, 256), 256)
            qkv[:, lanes] = matmul(xg[...], wqkv[:, lanes]).astype(BF16)
            return carry

        lax.fori_loop(0, 6, project, 0)

        for t in range(GROUPS):
            rows = slice(t * 64, (t + 1) * 64)
            for q in range(QUADS):
                lanes = slice(q * 128, (q + 1) * 128)
                query = qkv[rows, lanes]
                keys = qkv[rows, 512 + q * 128 : 640 + q * 128]
                values = qkv[rows, 1024 + q * 128 : 1152 + q * 128]
                apart = jnp.concatenate([query * one_hot(own_lanes[h]) for h in range(4)], axis=0)
                scores = lax.dot_general(
                    keys, apart, (((1,), (1,)), ((), ())), preferred_element_type=F32
                )
                scores = scores * (32**-0.5 * LOG2E) + bias[q]
                powers = jnp.exp2(scores - jnp.max(scores, axis=0, keepdims=True))
                share = 1.0 / jnp.sum(powers, axis=0, keepdims=True)
                attention = (powers * share).astype(BF16)
                mixed = lax.dot_general(
                    attention, values, (((0,), (0,)), ((), ())), preferred_element_type=F32
                )
                total = jnp.where(own_lanes[0], mixed[0:64], 0.0)
                for h in range(1, 4):
                    total = jnp.where(own_lanes[h], mixed[h * 64 : (h + 1) * 64], total)
                context[rows, lanes] = total.astype(BF16)

        answers[p] = reorder(2, context[...])
        exchange(2, p, answers, mid_back, along_cols, c)

        @pl.when(p < PARTS - 1)
        def _():
            pass_on(p + 1)

        wait_all(mid_back, p, received.at[2, p])
        mid_return[p] = reorder(0, mid_back[p])
        exchange(3, p, mid_return, returned, along_rows, a)
        return carry

    lax.fori_loop(0, PARTS, attend, 0)
    loads[9].wait()

    def written(p):
        f, first = p // 2, (p % 2) * PART_ROWS
        return pltpu.make_async_copy(
            ob.at[p], out_hbm.at[f, pl.ds(first, PART_ROWS)], out_sem.at[p]
        )

    def finish(p, carry):
        wait_all(returned, p, received.at[3, p])
        for i in range(2):
            lanes = slice(i * 256, (i + 1) * 256)
            total = conv[p, :, lanes].astype(F32) + matmul(returned[p], wo[:, lanes])
            ob[p, :, :, lanes] = total.astype(BF16).reshape(PART_ROWS, COLS, 256)
        written(p).start()
        return carry

    lax.fori_loop(0, PARTS, finish, 0)

    for copy in halos:
        copy.wait_send()

    def drain(p, carry):
        for stage, ref in enumerate((att, mid_out, answers, mid_return)):
            wait_all(ref, p, sent.at[stage, p])
        written(p).wait()
        return carry

    lax.fori_loop(0, PARTS, drain, 0)


def on_device(
    atmosphere_variables,
    premix_gain_vector,
    expand_weight,
    depth_weight,
    depth_bias,
    project_weight,
    norm_attn,
    qkv_weight,
    out_weight,
    bias_table,
):
    whole = pl.BlockSpec(memory_space=pltpu.HBM)
    tile = (FORECASTS, ROWS, COLS, WIDTH)
    parts = pltpu.VMEM((PARTS, PART, WIDTH), BF16)
    return pl.pallas_call(
        kernel,
        out_shape=jax.ShapeDtypeStruct(tile, BF16),
        in_specs=[whole] * 10,
        out_specs=pl.BlockSpec(memory_space=pl.ANY),
        scratch_shapes=[
            pltpu.VMEM(tile, BF16),
            pltpu.VMEM((1, WIDTH), F32),
            pltpu.VMEM((WIDTH, INNER), BF16),
            pltpu.VMEM((3, 3, INNER), F32),
            pltpu.VMEM((1, INNER), F32),
            pltpu.VMEM((INNER, WIDTH), BF16),
            pltpu.VMEM((1, WIDTH), F32),
            pltpu.VMEM((WIDTH, 3 * WIDTH), BF16),
            pltpu.VMEM((WIDTH, WIDTH), BF16),
            pltpu.VMEM((15, 16, 15), F32),
            pltpu.VMEM((6, 16, WIDTH), BF16),
            pltpu.VMEM((2, FORECASTS, COLS, WIDTH), BF16),
            pltpu.VMEM((6, 16, WIDTH), BF16),
            pltpu.VMEM((CELLS, WIDTH), BF16),
            pltpu.VMEM((FORECASTS, ROWS + 2, PADDED, INNER), F32),
            pltpu.VMEM((PART, INNER), BF16),
            *[parts] * 9,
            pltpu.VMEM((3, PART, PART), BF16),
            pltpu.VMEM((PART, WIDTH), BF16),
            pltpu.VMEM((PART, 3 * WIDTH), BF16),
            pltpu.VMEM((PART, WIDTH), BF16),
            pltpu.VMEM((16, 256), F32),
            pltpu.VMEM((16, MEMBERS, 128), F32),
            pltpu.VMEM((QUADS, MEMBERS, 256), F32),
            pltpu.VMEM((PARTS, PART_ROWS, COLS, WIDTH), BF16),
            pltpu.SemaphoreType.DMA((10,)),
            pltpu.SemaphoreType.DMA((8,)),
            pltpu.SemaphoreType.DMA((8,)),
            pltpu.SemaphoreType.DMA((4, PARTS)),
            pltpu.SemaphoreType.DMA((4, PARTS)),
            pltpu.SemaphoreType.DMA((PARTS,)),
        ],
        compiler_params=pltpu.CompilerParams(
            collective_id=0, has_side_effects=True, vmem_limit_bytes=56 * 1024 * 1024
        ),
        name="maxvit_layer",
    )(
        atmosphere_variables,
        premix_gain_vector.reshape(1, WIDTH),
        expand_weight,
        depth_weight,
        depth_bias.reshape(1, INNER),
        project_weight,
        norm_attn.reshape(1, WIDTH),
        qkv_weight,
        out_weight,
        bias_table.transpose(1, 0, 2),
    )


def solution(mesh):
    return jax.shard_map(
        on_device,
        mesh=mesh,
        in_specs=(P(None, "rows", "cols", None), P(), P(), P(), P(), P(), P(), P(), P(), P()),
        out_specs=P(None, "rows", "cols", None),
        check_vma=False,
    )
```

time: 92.1 us -> 82.2 us (0.89)
  the two profiles are of different devices: /device:TPU:1 before, /device:TPU:2 now
where the time goes in v2:
time: 82.2 us; the launch traced here: 82 us
  Pallas kernels  80.1 us (97%)
  local copies, waits for them, and re-layouts  1.88 us (2%)
    pallas_call x1, Pallas kernels, on_device(): pl.pallas_call(kernel, out_shape=jax.ShapeDtypeStruct(tile, BF16), in_spe...  80.1 us
    unnamed x1, local copies, waits for them, and re-layouts  1.88 us

profile of v2, /device:TPU:2, one launch (start us, length us, event | category | flops | bytes accessed | tf_op | source)
XLA Modules:
  0.0 82.0 jit_solution(5994510004020934857)
XLA Ops:
  0.0 80.1 %maxvit_layer.1 = bf16[2,8,32,512]{3,2,1,0:T(8,128)(2,1)} custom-call(bf16[2,8,32,512]{3,2,1,0:T(8,128)(2,1)} %x_hbm.1, f32[1,512]{1,0:T(1,128)} %bitcast.6, bf16[512,1024]{1,0:T(8,128)(2,1)} %we_hbm.1, f32[3,3,1024]{2,1,0:T(4,128)} %dw_hbm.1, f32[1,1024]{1,0:T(1,128)} %bitcast.5, bf16[1024,512]{1,0:T(8,128)(2,1)} %wp_hbm.1, f32[1,512]{1,0:T(1,128)} %bitcast.7, ...), custom_call_target="tpu_custom_call" | custom-call | tf_op jit(solution)/shard_map/maxvit_layer/pallas_call | solution.py:400
  80.1 1.9 %copy.12 = bf16[2,8,32,512]{3,2,1,0:T(8,128)(2,1)} copy(bf16[2,8,32,512]{3,2,1,0:T(8,128)(2,1)} %maxvit_layer.1) | data formatting | bytes 1048576

commit v3 on v2

--- a/solution.py
+++ b/solution.py
@@ -17,8 +17,8 @@
 INNER = 1024
 SIDE = 8
 PARTS = 4
-PART_ROWS = FORECASTS * ROWS // PARTS
-PART = PART_ROWS * COLS
+PART = FORECASTS * CELLS // PARTS
+INNER_ROWS = 5
 PIECE = PART // SIDE
 GROUPS = PIECE // SIDE
 MEMBERS = SIDE * SIDE
@@ -46,18 +46,27 @@
     return jnp.where(condition, 1.0, 0.0).astype(BF16)
 
 
+def cells_of(inner, k):
+    if inner:
+        return (1 + k // 30) * COLS + 1 + k % 30
+    edges = (1 + (k - 32) // 2) * COLS + (k - 32) % 2 * 31
+    fifth = 5 * COLS + jnp.where(k == 40, 0, k - 32)
+    last = 6 * COLS + k - 64
+    return jnp.where(k < 32, k, jnp.where(k < 40, edges, jnp.where(k < 64, fifth, last)))
+
+
 def matmul(a, b):
     return jnp.dot(a, b, preferred_element_type=F32)
 
 
 def kernel(
     x_hbm, premix_hbm, we_hbm, dw_hbm, db_hbm, wp_hbm, gain_hbm, wqkv_hbm, wo_hbm, table_hbm,
-    out_hbm,
+    out_ref,
     xb, premix_ref, we, dw_ref, db_ref, wp, gain_ref, wqkv, wo, table_ref,
-    edge, halo_rows, halo_edge, normed, ex, act, conv,
+    edge, halo_rows, halo_edge, normed, ex, act, chosen_act, conv, choose, restore, finished,
     att, mid, mid_out, owned, answers, mid_back, mid_return, returned,
-    orders, xg, qkv, context, flat, shifted, bias, ob,
-    load_sem, halo_send, halo_recv, sent, received, out_sem,
+    orders, xg, qkv, context, flat, shifted, bias,
+    load_sem, halo_send, halo_recv, sent, received,
 ):
     r = lax.axis_index("rows")
     c = lax.axis_index("cols")
@@ -69,13 +78,13 @@
         pltpu.make_async_copy(src, dst, load_sem.at[i])
         for i, (src, dst) in enumerate(
             (
-                (x_hbm, xb), (premix_hbm, premix_ref), (we_hbm, we), (dw_hbm, dw_ref),
+                (x_hbm.at[0], xb.at[0]), (premix_hbm, premix_ref), (we_hbm, we), (dw_hbm, dw_ref),
                 (db_hbm, db_ref), (wp_hbm, wp), (gain_hbm, gain_ref), (table_hbm, table_ref),
-                (wqkv_hbm, wqkv), (wo_hbm, wo),
+                (wqkv_hbm, wqkv), (wo_hbm, wo), (x_hbm.at[1], xb.at[1]),
             )
         )
     ]
-    for load in loads[:3]:
+    for load in loads[:3] + loads[10:]:
         load.start()
 
     north, south = lax.rem(r + n_rows - 1, n_rows), lax.rem(r + 1, n_rows)
@@ -101,19 +110,6 @@
         return carry
 
     lax.fori_loop(1, SIDE, greet, 0)
-
-    loads[0].wait()
-    for load in loads[3:]:
-        load.start()
-    place = iota((96, 512), 0)
-    piece, index = place // 16, place % 16
-    cell_f = jnp.where(piece < 2, index // 8, index % 2)
-    cell_y = jnp.where(piece < 2, index % 8, jnp.where(piece < 4, 0, 7))
-    cell_x = jnp.where(piece % 2 == 0, 0, 31)
-    chosen = iota((96, 512), 1) == cell_f * CELLS + cell_y * COLS + cell_x
-    edge[...] = matmul(one_hot(chosen), xb[...].reshape(512, WIDTH)).astype(BF16).reshape(6, 16, WIDTH)
-
-    pl.semaphore_wait(barrier, 2 * (SIDE - 1) + 6)
 
     def halo(i, src, dst, row, col):
         return pltpu.make_async_remote_copy(
@@ -135,9 +131,6 @@
         halo(6, edge.at[3], halo_edge.at[4], north, east),
         halo(7, edge.at[2], halo_edge.at[5], north, west),
     ]
-    for copy in halos:
-        copy.start()
-
     def block(k):
         return pl.ds(pl.multiple_of(k * PIECE, PIECE), PIECE)
 
@@ -161,11 +154,7 @@
         others = ref.at[p, pl.ds(0, PART - PIECE)]
         pltpu.make_async_copy(others, others, sem).wait()
 
-    loads[1].wait()
-    premix = premix_ref[...]
-    loads[2].wait()
-
-    def expand_tile(f, carry):
+    def expand_tile(f):
         def norm_rows(i, carry):
             v = xb[f, pl.ds(2 * i, 2)].astype(F32).reshape(64, WIDTH)
             normed[pl.ds(pl.multiple_of(i * 64, 64), 64)] = layer_norm(v, premix).astype(BF16)
@@ -180,12 +169,34 @@
             return carry
 
         lax.fori_loop(0, INNER // 256, expand, 0)
-        return carry
-
-    lax.fori_loop(0, FORECASTS, expand_tile, 0)
-
+
+    for f in range(FORECASTS):
+        ex[f, :, COLS:PADDED] = jnp.zeros((ROWS + 2, PADDED - COLS, INNER), F32)
+    for i in range(2):
+        place, cell = iota((PART, CELLS), 0), iota((PART, CELLS), 1)
+        choose[i] = one_hot(cell == cells_of(i == 0, place))
+        place, cell = iota((CELLS, PART), 1), iota((CELLS, PART), 0)
+        restore[i] = one_hot(cell == cells_of(i == 0, place))
+    loads[0].wait()
+    loads[1].wait()
+    premix = premix_ref[...]
+    loads[2].wait()
+    for load in loads[3:10]:
+        load.start()
+    expand_tile(0)
+
+    loads[10].wait()
+    place = iota((96, 512), 0)
+    piece, index = place // 16, place % 16
+    cell_f = jnp.where(piece < 2, index // 8, index % 2)
+    cell_y = jnp.where(piece < 2, index % 8, jnp.where(piece < 4, 0, 7))
+    cell_x = jnp.where(piece % 2 == 0, 0, 31)
+    chosen = iota((96, 512), 1) == cell_f * CELLS + cell_y * COLS + cell_x
+    edge[...] = matmul(one_hot(chosen), xb[...].reshape(512, WIDTH)).astype(BF16).reshape(6, 16, WIDTH)
+
+    pl.semaphore_wait(barrier, 2 * (SIDE - 1) + 6)
     for copy in halos:
-        copy.wait_recv()
+        copy.start()
     for load in loads[3:7]:
         load.wait()
     gain = gain_ref[...]
@@ -217,38 +228,59 @@
 
         lax.fori_loop(0, INNER // 256, expand, 0)
 
-    def convolve(p, carry):
-        f, first = p // 2, (p % 2) * PART_ROWS
-
-        @pl.when(p % 2 == 0)
-        def _():
-            expand_halo(f)
-
-        def filter_row(y, carry):
-            for i in range(INNER // 256):
-                lanes = slice(i * 256, (i + 1) * 256)
-                around = [ex[f, first + y + q, :, lanes] for q in range(3)]
-                taps = [
-                    sum(around[q] * dw_ref[q, s : s + 1, lanes] for q in range(3)) for s in range(3)
-                ]
-                total = pltpu.roll(taps[0], 1, 0) + taps[1] + pltpu.roll(taps[2], PADDED - 1, 0)
-                act[pl.ds(pl.multiple_of(y * COLS, COLS), COLS), lanes] = gelu(
-                    total[0:COLS] + db_ref[:, lanes]
-                ).astype(BF16)
+    def filter_row(f, y):
+        for i in range(INNER // 256):
+            lanes = slice(i * 256, (i + 1) * 256)
+            around = [ex[f, y + q, :, lanes] for q in range(3)]
+            taps = [
+                sum(around[q] * dw_ref[q, s : s + 1, lanes] for q in range(3)) for s in range(3)
+            ]
+            total = pltpu.roll(taps[0], 1, 0) + taps[1] + pltpu.roll(taps[2], PADDED - 1, 0)
+            act[pl.ds(pl.multiple_of(y * COLS, COLS), COLS), lanes] = gelu(
+                total[0:COLS] + db_ref[:, lanes]
+            ).astype(BF16)
+
+    def convolve(f, inner, p):
+        first, last = (1, 1 + INNER_ROWS) if inner else (0, ROWS)
+
+        def filter_rows(y, carry):
+            filter_row(f, y)
             return carry
 
-        lax.fori_loop(0, PART_ROWS, filter_row, 0)
+        lax.fori_loop(first, last, filter_rows, 0)
+        cells = slice(first * COLS, last * COLS)
+        kind = 0 if inner else 1
+        for i in range(2):
+            lanes = slice(i * 512, (i + 1) * 512)
+            chosen_act[:, lanes] = matmul(choose[kind, :, cells], act[cells, lanes]).astype(BF16)
         for i in range(2):
             lanes = slice(i * 256, (i + 1) * 256)
-            residual = xb[f, pl.ds(first, PART_ROWS), :, lanes].astype(F32).reshape(PART, 256)
-            conv[p, :, lanes] = (residual + matmul(act[...], wp[:, lanes])).astype(BF16)
+            residual = matmul(choose[kind], xb[f, :, :, lanes].reshape(CELLS, 256))
+            conv[p, :, lanes] = (residual + matmul(chosen_act[...], wp[:, lanes])).astype(BF16)
         for i in range(2):
             rows = slice(i * 64, (i + 1) * 64)
             att[p, rows] = layer_norm(conv[p, rows].astype(F32), gain).astype(BF16)
         exchange(0, p, att, mid, along_rows, a)
-        return carry
-
-    lax.fori_loop(0, PARTS, convolve, 0)
+
+    def convolve_inner(f, carry):
+        @pl.when(f > 0)
+        def _():
+            expand_tile(f)
+
+        convolve(f, True, f)
+        return carry
+
+    lax.fori_loop(0, FORECASTS, convolve_inner, 0)
+
+    for copy in halos:
+        copy.wait_recv()
+
+    def convolve_outer(f, carry):
+        expand_halo(f)
+        convolve(f, False, FORECASTS + f)
+        return carry
+
+    lax.fori_loop(0, FORECASTS, convolve_outer, 0)
 
     row, col = iota((PART, PART), 0), iota((PART, PART), 1)
     swapped = row // 16 * 2 + row % 16 // 2 * 16 + row % 2
@@ -304,7 +336,7 @@
     head = iota((1, 128), 1) // 32
     own_lanes = [head == h for h in range(4)]
 
-    def attend(p, carry):
+    def attend(p):
         wait_all(owned, p, received.at[1, p])
         xg[...] = reorder(1, owned[p])
 
@@ -341,31 +373,47 @@
         answers[p] = reorder(2, context[...])
         exchange(2, p, answers, mid_back, along_cols, c)
 
-        @pl.when(p < PARTS - 1)
-        def _():
-            pass_on(p + 1)
-
+    def pass_back(p):
         wait_all(mid_back, p, received.at[2, p])
         mid_return[p] = reorder(0, mid_back[p])
         exchange(3, p, mid_return, returned, along_rows, a)
-        return carry
-
-    lax.fori_loop(0, PARTS, attend, 0)
+
+    def step(i, carry):
+        @pl.when(i < PARTS)
+        def _():
+            pass_on(i)
+
+        @pl.when(i <= PARTS)
+        def _():
+            attend(i - 1)
+
+        @pl.when(i >= 2)
+        def _():
+            pass_back(i - 2)
+
+        return carry
+
+    lax.fori_loop(1, PARTS + 2, step, 0)
     loads[9].wait()
-
-    def written(p):
-        f, first = p // 2, (p % 2) * PART_ROWS
-        return pltpu.make_async_copy(
-            ob.at[p], out_hbm.at[f, pl.ds(first, PART_ROWS)], out_sem.at[p]
-        )
 
     def finish(p, carry):
         wait_all(returned, p, received.at[3, p])
+        f, kind = p % FORECASTS, p // FORECASTS
         for i in range(2):
             lanes = slice(i * 256, (i + 1) * 256)
             total = conv[p, :, lanes].astype(F32) + matmul(returned[p], wo[:, lanes])
-            ob[p, :, :, lanes] = total.astype(BF16).reshape(PART_ROWS, COLS, 256)
-        written(p).start()
+            placed = matmul(restore[kind], total.astype(BF16))
+
+            @pl.when(kind == 0)
+            def _():
+                finished[f, :, lanes] = placed
+
+            @pl.when(kind == 1)
+            def _():
+                out_ref[f, :, :, lanes] = (
+                    (finished[f, :, lanes] + placed).astype(BF16).reshape(ROWS, COLS, 256)
+                )
+
         return carry
 
     lax.fori_loop(0, PARTS, finish, 0)
@@ -376,7 +424,6 @@
     def drain(p, carry):
         for stage, ref in enumerate((att, mid_out, answers, mid_return)):
             wait_all(ref, p, sent.at[stage, p])
-        written(p).wait()
         return carry
 
     lax.fori_loop(0, PARTS, drain, 0)
@@ -399,9 +446,9 @@
     parts = pltpu.VMEM((PARTS, PART, WIDTH), BF16)
     return pl.pallas_call(
         kernel,
-        out_shape=jax.ShapeDtypeStruct(tile, BF16),
+        out_shape=pltpu.VMEM(tile, BF16),
         in_specs=[whole] * 10,
-        out_specs=pl.BlockSpec(memory_space=pl.ANY),
+        out_specs=pl.BlockSpec(memory_space=pltpu.VMEM),
         scratch_shapes=[
             pltpu.VMEM(tile, BF16),
             pltpu.VMEM((1, WIDTH), F32),
@@ -418,8 +465,13 @@
             pltpu.VMEM((6, 16, WIDTH), BF16),
             pltpu.VMEM((CELLS, WIDTH), BF16),
             pltpu.VMEM((FORECASTS, ROWS + 2, PADDED, INNER), F32),
+            pltpu.VMEM((CELLS, INNER), BF16),
             pltpu.VMEM((PART, INNER), BF16),
-            *[parts] * 9,
+            parts,
+            pltpu.VMEM((2, PART, CELLS), BF16),
+            pltpu.VMEM((2, CELLS, PART), BF16),
+            pltpu.VMEM((FORECASTS, CELLS, WIDTH), F32),
+            *[parts] * 8,
             pltpu.VMEM((3, PART, PART), BF16),
             pltpu.VMEM((PART, WIDTH), BF16),
             pltpu.VMEM((PART, 3 * WIDTH), BF16),
@@ -427,13 +479,11 @@
             pltpu.VMEM((16, 256), F32),
             pltpu.VMEM((16, MEMBERS, 128), F32),
             pltpu.VMEM((QUADS, MEMBERS, 256), F32),
-            pltpu.VMEM((PARTS, PART_ROWS, COLS, WIDTH), BF16),
-            pltpu.SemaphoreType.DMA((10,)),
+            pltpu.SemaphoreType.DMA((11,)),
             pltpu.SemaphoreType.DMA((8,)),
             pltpu.SemaphoreType.DMA((8,)),
             pltpu.SemaphoreType.DMA((4, PARTS)),
             pltpu.SemaphoreType.DMA((4, PARTS)),
-            pltpu.SemaphoreType.DMA((PARTS,)),
         ],
         compiler_params=pltpu.CompilerParams(
             collective_id=0, has_side_effects=True, vmem_limit_bytes=56 * 1024 * 1024

time: 82.2 us -> 73.5 us (0.89)
  Pallas kernels: 80.1 us -> 72.6 us
  local copies, waits for them, and re-layouts: 1.88 us -> 0.8 us
    pallas_call x1, Pallas kernels: 80.1 us -> 72.6 us  [on_device(): pl.pallas_call(kernel, out_shape=pltpu.VMEM(tile, BF16), in_specs=[whole]...]
    unnamed x1, local copies, waits for them, and re-layouts: 1.88 us -> 0.8 us
where the time goes in v3:
time: 73.5 us; the launch traced here: 73.4 us
  Pallas kernels  72.6 us (99%)
  local copies, waits for them, and re-layouts  0.8 us (1%)
    pallas_call x1, Pallas kernels, on_device(): pl.pallas_call(kernel, out_shape=pltpu.VMEM(tile, BF16), in_specs=[whole]...  72.6 us

profile of v3, /device:TPU:2, one launch (start us, length us, event | category | flops | bytes accessed | tf_op | source)
XLA Modules:
  0.0 73.4 jit_solution(8179074632015049426)
XLA Ops:
  0.0 72.6 %maxvit_layer.1 = bf16[2,8,32,512]{3,2,1,0:T(8,128)(2,1)S(1)} custom-call(bf16[2,8,32,512]{3,2,1,0:T(8,128)(2,1)} %x_hbm.1, f32[1,512]{1,0:T(1,128)} %bitcast.6, bf16[512,1024]{1,0:T(8,128)(2,1)} %we_hbm.1, f32[3,3,1024]{2,1,0:T(4,128)} %dw_hbm.1, f32[1,1024]{1,0:T(1,128)} %bitcast.5, bf16[1024,512]{1,0:T(8,128)(2,1)} %wp_hbm.1, f32[1,512]{1,0:T(1,128)} %bitcast.7, ...), custom_call_target="tpu_custom_call" | custom-call | tf_op jit(solution)/shard_map/maxvit_layer/pallas_call | solution.py:447
  72.6 0.8 %copy.12 = bf16[2,8,32,512]{3,2,1,0:T(8,128)(2,1)} copy(bf16[2,8,32,512]{3,2,1,0:T(8,128)(2,1)S(1)} %maxvit_layer.1) | data formatting | bytes 1048576

commit v4 on v3

--- a/solution.py
+++ b/solution.py
@@ -46,13 +46,16 @@
     return jnp.where(condition, 1.0, 0.0).astype(BF16)
 
 
-def cells_of(inner, k):
+def place_of(inner, cell):
+    y, x = cell >> 5, cell & 31
     if inner:
-        return (1 + k // 30) * COLS + 1 + k % 30
-    edges = (1 + (k - 32) // 2) * COLS + (k - 32) % 2 * 31
-    fifth = 5 * COLS + jnp.where(k == 40, 0, k - 32)
-    last = 6 * COLS + k - 64
-    return jnp.where(k < 32, k, jnp.where(k < 40, edges, jnp.where(k < 64, fifth, last)))
+        k = (y - 1) * 30 + x - 1
+        return jnp.where((y > 0) & (y < 6) & (x > 0) & (x < 31) & (k < PART), k, -1)
+    sides = jnp.where(x == 0, 2 * y + 30, jnp.where(x == 31, 2 * y + 31, -1))
+    fifth = jnp.where(x == 0, 40, jnp.where(x > 8, 32 + x, -1))
+    return jnp.where(
+        y == 0, x, jnp.where(y < 5, sides, jnp.where(y == 5, fifth, cell - (CELLS - PART)))
+    )
 
 
 def matmul(a, b):
@@ -160,7 +163,7 @@
             normed[pl.ds(pl.multiple_of(i * 64, 64), 64)] = layer_norm(v, premix).astype(BF16)
             return carry
 
-        lax.fori_loop(0, 4, norm_rows, 0)
+        lax.fori_loop(0, 4, norm_rows, 0, unroll=True)
 
         def expand(i, carry):
             lanes = pl.ds(pl.multiple_of(i * 256, 256), 256)
@@ -168,15 +171,12 @@
             ex[f, 1 : ROWS + 1, 0:COLS, lanes] = g.reshape(ROWS, COLS, 256)
             return carry
 
-        lax.fori_loop(0, INNER // 256, expand, 0)
+        lax.fori_loop(0, INNER // 256, expand, 0, unroll=True)
 
     for f in range(FORECASTS):
         ex[f, :, COLS:PADDED] = jnp.zeros((ROWS + 2, PADDED - COLS, INNER), F32)
     for i in range(2):
-        place, cell = iota((PART, CELLS), 0), iota((PART, CELLS), 1)
-        choose[i] = one_hot(cell == cells_of(i == 0, place))
-        place, cell = iota((CELLS, PART), 1), iota((CELLS, PART), 0)
-        restore[i] = one_hot(cell == cells_of(i == 0, place))
+        choose[i] = one_hot(iota((PART, CELLS), 0) == place_of(i == 0, iota((1, CELLS), 1)))
     loads[0].wait()
     loads[1].wait()
     premix = premix_ref[...]
@@ -186,11 +186,11 @@
     expand_tile(0)
 
     loads[10].wait()
-    place = iota((96, 512), 0)
-    piece, index = place // 16, place % 16
-    cell_f = jnp.where(piece < 2, index // 8, index % 2)
-    cell_y = jnp.where(piece < 2, index % 8, jnp.where(piece < 4, 0, 7))
-    cell_x = jnp.where(piece % 2 == 0, 0, 31)
+    place = iota((96, 1), 0)
+    piece, index = place >> 4, place & 15
+    cell_f = jnp.where(piece < 2, index >> 3, index & 1)
+    cell_y = jnp.where(piece < 2, index & 7, jnp.where(piece < 4, 0, 7))
+    cell_x = (piece & 1) * 31
     chosen = iota((96, 512), 1) == cell_f * CELLS + cell_y * COLS + cell_x
     edge[...] = matmul(one_hot(chosen), xb[...].reshape(512, WIDTH)).astype(BF16).reshape(6, 16, WIDTH)
 
@@ -206,15 +206,16 @@
         bottom = halo_rows[1, f].astype(F32) * jnp.where(r == n_rows - 1, 0.0, 1.0)
         normed[0:32] = layer_norm(top, premix).astype(BF16)
         normed[32:64] = layer_norm(bottom, premix).astype(BF16)
-        place = iota((80, 96), 0)
-        y, slot = place // 8, place % 8
+        place = iota((80, 1), 0)
+        y, slot = place >> 3, place & 7
         inside = ((y > 0) | (r > 0)) & ((y < 9) | (r < n_rows - 1))
         in_east = (slot == 0) & (c < n_cols - 1)
         in_west = (slot == 7) & (c > 0)
         source_east = jnp.where(y == 0, 48 + f, jnp.where(y == 9, 80 + f, f * 8 + y - 1))
         source_west = jnp.where(y == 0, 32 + f, jnp.where(y == 9, 64 + f, 16 + f * 8 + y - 1))
         source = jnp.where(in_east, source_east, source_west)
-        chosen = (iota((80, 96), 1) == source) & inside & (in_east | in_west)
+        source = jnp.where(inside & (in_east | in_west), source, -1)
+        chosen = iota((80, 96), 1) == source
         sides = matmul(one_hot(chosen), halo_edge[...].reshape(96, WIDTH))
         normed[64:144] = layer_norm(sides, premix).astype(BF16)
 
@@ -226,7 +227,7 @@
             ex[f, :, COLS:PADDED, lanes] = g[64:144].reshape(ROWS + 2, 8, 256)
             return carry
 
-        lax.fori_loop(0, INNER // 256, expand, 0)
+        lax.fori_loop(0, INNER // 256, expand, 0, unroll=True)
 
     def filter_row(f, y):
         for i in range(INNER // 256):
@@ -282,13 +283,10 @@
 
     lax.fori_loop(0, FORECASTS, convolve_outer, 0)
 
-    row, col = iota((PART, PART), 0), iota((PART, PART), 1)
-    swapped = row // 16 * 2 + row % 16 // 2 * 16 + row % 2
-    orders[0] = one_hot(col == swapped)
-    grouped = row % 8 * 16 + row % 64 // 8 * 2 + row // 64
-    orders[1] = one_hot(col == grouped)
-    ungrouped = row % 2 * 64 + row % 16 // 2 * 8 + row // 16
-    orders[2] = one_hot(col == ungrouped)
+    row, col = iota((PART, 1), 0), iota((PART, PART), 1)
+    orders[0] = one_hot(col == ((row >> 4) << 1) + (((row & 15) >> 1) << 4) + (row & 1))
+    orders[1] = one_hot(col == ((row & 7) << 4) + (((row & 63) >> 3) << 1) + (row >> 6))
+    orders[2] = one_hot(col == ((row & 1) << 6) + (((row & 15) >> 1) << 3) + (row >> 4))
 
     def reorder(i, v):
         return matmul(orders[i], v).astype(BF16)
@@ -315,10 +313,10 @@
             shifted[h, i * 8 : (i + 1) * 8] = moved[:, 0:128]
         return carry
 
-    lax.fori_loop(0, 16, shift, 0)
-    source, target = iota((512, 256), 0), iota((512, 256), 1)
-    member = target % 64
-    spread = one_hot(source == (target // 64) * 128 + 16 * (member // 8) + member % 8)
+    lax.fori_loop(0, 16, shift, 0, unroll=True)
+    target = iota((1, 256), 1)
+    lane = ((target >> 6) << 7) + (((target & 63) >> 3) << 4) + (target & 7)
+    spread = one_hot(iota((512, 256), 0) == lane)
 
     def set_bias(q, carry):
         rest = jnp.concatenate([shifted[q * 4 + h] for h in range(4)], axis=1)
@@ -333,7 +331,7 @@
     lax.fori_loop(0, QUADS, set_bias, 0)
     loads[8].wait()
 
-    head = iota((1, 128), 1) // 32
+    head = iota((1, 128), 1) >> 5
     own_lanes = [head == h for h in range(4)]
 
     def attend(p):
@@ -345,7 +343,7 @@
             qkv[:, lanes] = matmul(xg[...], wqkv[:, lanes]).astype(BF16)
             return carry
 
-        lax.fori_loop(0, 6, project, 0)
+        lax.fori_loop(0, 6, project, 0, unroll=True)
 
         for t in range(GROUPS):
             rows = slice(t * 64, (t + 1) * 64)
@@ -376,7 +374,23 @@
     def pass_back(p):
         wait_all(mid_back, p, received.at[2, p])
         mid_return[p] = reorder(0, mid_back[p])
-        exchange(3, p, mid_return, returned, along_rows, a)
+
+        def send(k, carry):
+            @pl.when(k != a)
+            def _():
+                pltpu.make_async_remote_copy(
+                    src_ref=mid_return.at[p, block(k)],
+                    dst_ref=returned.at[p, block(a)],
+                    send_sem=sent.at[3, p],
+                    recv_sem=received.at[3, p],
+                    device_id=(k * SIDE + m, c),
+                    device_id_type=MESH,
+                ).start()
+
+            return carry
+
+        lax.fori_loop(0, SIDE, send, 0)
+        returned[p, block(a)] = mid_return[p, block(a)]
 
     def step(i, carry):
         @pl.when(i < PARTS)
@@ -395,6 +409,8 @@
 
     lax.fori_loop(1, PARTS + 2, step, 0)
     loads[9].wait()
+    for i in range(2):
+        restore[i] = one_hot(iota((CELLS, PART), 1) == place_of(i == 0, iota((CELLS, 1), 0)))
 
     def finish(p, carry):
         wait_all(returned, p, received.at[3, p])

time: 73.5 us -> 69.8 us (0.950)
  the two profiles are of different devices: /device:TPU:2 before, /device:TPU:4 now
where the time goes in v4:
time: 69.8 us; the launch traced here: 69.7 us
  Pallas kernels  68.9 us (99%)
  local copies, waits for them, and re-layouts  0.8 us (1%)
    pallas_call x1, Pallas kernels, on_device(): pl.pallas_call(kernel, out_shape=pltpu.VMEM(tile, BF16), in_specs=[whole]...  68.9 us

profile of v4, /device:TPU:4, one launch (start us, length us, event | category | flops | bytes accessed | tf_op | source)
XLA Modules:
  0.0 69.7 jit_solution(4471426300375937814)
XLA Ops:
  0.0 68.9 %maxvit_layer.1 = bf16[2,8,32,512]{3,2,1,0:T(8,128)(2,1)S(1)} custom-call(bf16[2,8,32,512]{3,2,1,0:T(8,128)(2,1)} %x_hbm.1, f32[1,512]{1,0:T(1,128)} %bitcast.6, bf16[512,1024]{1,0:T(8,128)(2,1)} %we_hbm.1, f32[3,3,1024]{2,1,0:T(4,128)} %dw_hbm.1, f32[1,1024]{1,0:T(1,128)} %bitcast.5, bf16[1024,512]{1,0:T(8,128)(2,1)} %wp_hbm.1, f32[1,512]{1,0:T(1,128)} %bitcast.7, ...), custom_call_target="tpu_custom_call" | custom-call | tf_op jit(solution)/shard_map/maxvit_layer/pallas_call | solution.py:463
  68.9 0.8 %copy.12 = bf16[2,8,32,512]{3,2,1,0:T(8,128)(2,1)} copy(bf16[2,8,32,512]{3,2,1,0:T(8,128)(2,1)S(1)} %maxvit_layer.1) | data formatting | bytes 1048576

commit v5 on v4

--- a/solution.py
+++ b/solution.py
@@ -87,7 +87,7 @@
             )
         )
     ]
-    for load in loads[:3] + loads[10:]:
+    for load in loads[:3]:
         load.start()
 
     north, south = lax.rem(r + n_rows - 1, n_rows), lax.rem(r + 1, n_rows)
@@ -178,25 +178,12 @@
     for i in range(2):
         choose[i] = one_hot(iota((PART, CELLS), 0) == place_of(i == 0, iota((1, CELLS), 1)))
     loads[0].wait()
+    for load in loads[3:]:
+        load.start()
     loads[1].wait()
     premix = premix_ref[...]
     loads[2].wait()
-    for load in loads[3:10]:
-        load.start()
     expand_tile(0)
-
-    loads[10].wait()
-    place = iota((96, 1), 0)
-    piece, index = place >> 4, place & 15
-    cell_f = jnp.where(piece < 2, index >> 3, index & 1)
-    cell_y = jnp.where(piece < 2, index & 7, jnp.where(piece < 4, 0, 7))
-    cell_x = (piece & 1) * 31
-    chosen = iota((96, 512), 1) == cell_f * CELLS + cell_y * COLS + cell_x
-    edge[...] = matmul(one_hot(chosen), xb[...].reshape(512, WIDTH)).astype(BF16).reshape(6, 16, WIDTH)
-
-    pl.semaphore_wait(barrier, 2 * (SIDE - 1) + 6)
-    for copy in halos:
-        copy.start()
     for load in loads[3:7]:
         load.wait()
     gain = gain_ref[...]
@@ -261,17 +248,24 @@
         for i in range(2):
             rows = slice(i * 64, (i + 1) * 64)
             att[p, rows] = layer_norm(conv[p, rows].astype(F32), gain).astype(BF16)
-        exchange(0, p, att, mid, along_rows, a)
-
-    def convolve_inner(f, carry):
-        @pl.when(f > 0)
-        def _():
-            expand_tile(f)
-
-        convolve(f, True, f)
-        return carry
-
-    lax.fori_loop(0, FORECASTS, convolve_inner, 0)
+
+    convolve(0, True, 0)
+    pl.semaphore_wait(barrier, 2 * (SIDE - 1) + 6)
+    exchange(0, 0, att, mid, along_rows, a)
+
+    loads[10].wait()
+    place = iota((96, 1), 0)
+    piece, index = place >> 4, place & 15
+    cell_f = jnp.where(piece < 2, index >> 3, index & 1)
+    cell_y = jnp.where(piece < 2, index & 7, jnp.where(piece < 4, 0, 7))
+    cell_x = (piece & 1) * 31
+    chosen = iota((96, 512), 1) == cell_f * CELLS + cell_y * COLS + cell_x
+    edge[...] = matmul(one_hot(chosen), xb[...].reshape(512, WIDTH)).astype(BF16).reshape(6, 16, WIDTH)
+    for copy in halos:
+        copy.start()
+    expand_tile(1)
+    convolve(1, True, 1)
+    exchange(0, 1, att, mid, along_rows, a)
 
     for copy in halos:
         copy.wait_recv()
@@ -279,6 +273,7 @@
     def convolve_outer(f, carry):
         expand_halo(f)
         convolve(f, False, FORECASTS + f)
+        exchange(0, FORECASTS + f, att, mid, along_rows, a)
         return carry
 
     lax.fori_loop(0, FORECASTS, convolve_outer, 0)

time: 69.8 us -> 68.8 us (0.986)
  the two profiles are of different devices: /device:TPU:4 before, /device:TPU:5 now
where the time goes in v5:
time: 68.8 us; the launch traced here: 68.6 us
  Pallas kernels  67.8 us (99%)
  local copies, waits for them, and re-layouts  0.8 us (1%)
    pallas_call x1, Pallas kernels, on_device(): pl.pallas_call(kernel, out_shape=pltpu.VMEM(tile, BF16), in_specs=[whole]...  67.8 us

profile of v5, /device:TPU:5, one launch (start us, length us, event | category | flops | bytes accessed | tf_op | source)
XLA Modules:
  0.0 68.6 jit_solution(18128049104443004139)
XLA Ops:
  0.0 67.8 %maxvit_layer.1 = bf16[2,8,32,512]{3,2,1,0:T(8,128)(2,1)S(1)} custom-call(bf16[2,8,32,512]{3,2,1,0:T(8,128)(2,1)} %x_hbm.1, f32[1,512]{1,0:T(1,128)} %bitcast.6, bf16[512,1024]{1,0:T(8,128)(2,1)} %we_hbm.1, f32[3,3,1024]{2,1,0:T(4,128)} %dw_hbm.1, f32[1,1024]{1,0:T(1,128)} %bitcast.5, bf16[1024,512]{1,0:T(8,128)(2,1)} %wp_hbm.1, f32[1,512]{1,0:T(1,128)} %bitcast.7, ...), custom_call_target="tpu_custom_call" | custom-call | tf_op jit(solution)/shard_map/maxvit_layer/pallas_call | solution.py:458
  67.8 0.8 %copy.12 = bf16[2,8,32,512]{3,2,1,0:T(8,128)(2,1)} copy(bf16[2,8,32,512]{3,2,1,0:T(8,128)(2,1)S(1)} %maxvit_layer.1) | data formatting | bytes 1048576

commit v6 on v5

--- a/solution.py
+++ b/solution.py
@@ -138,7 +138,8 @@
         return pl.ds(pl.multiple_of(k * PIECE, PIECE), PIECE)
 
     def exchange(stage, p, src, dst, along, mine):
-        def send(k, carry):
+        def send(n, carry):
+            k = SIDE // 2 + jnp.where(n % 2 == 1, -(n // 2), n // 2)
             other, place = along(k)
             pltpu.make_async_remote_copy(
                 src_ref=src.at[p, block(other)],
@@ -407,37 +408,39 @@
     for i in range(2):
         restore[i] = one_hot(iota((CELLS, PART), 1) == place_of(i == 0, iota((CELLS, 1), 0)))
 
+    for copy in halos:
+        copy.wait_send()
+
+    def drain(p, carry):
+        for stage, ref in enumerate((att, mid_out, answers)):
+            wait_all(ref, p, sent.at[stage, p])
+        return carry
+
+    lax.fori_loop(0, PARTS, drain, 0)
+
     def finish(p, carry):
         wait_all(returned, p, received.at[3, p])
         f, kind = p % FORECASTS, p // FORECASTS
-        for i in range(2):
-            lanes = slice(i * 256, (i + 1) * 256)
-            total = conv[p, :, lanes].astype(F32) + matmul(returned[p], wo[:, lanes])
-            placed = matmul(restore[kind], total.astype(BF16))
-
-            @pl.when(kind == 0)
-            def _():
-                finished[f, :, lanes] = placed
-
-            @pl.when(kind == 1)
-            def _():
-                out_ref[f, :, :, lanes] = (
-                    (finished[f, :, lanes] + placed).astype(BF16).reshape(ROWS, COLS, 256)
-                )
+        total = conv[p].astype(F32) + matmul(returned[p], wo[...])
+        placed = matmul(restore[kind], total.astype(BF16))
+
+        @pl.when(kind == 0)
+        def _():
+            finished[f] = placed
+
+        @pl.when(kind == 1)
+        def _():
+            out_ref[f] = (finished[f] + placed).astype(BF16).reshape(ROWS, COLS, WIDTH)
 
         return carry
 
     lax.fori_loop(0, PARTS, finish, 0)
 
-    for copy in halos:
-        copy.wait_send()
-
-    def drain(p, carry):
-        for stage, ref in enumerate((att, mid_out, answers, mid_return)):
-            wait_all(ref, p, sent.at[stage, p])
-        return carry
-
-    lax.fori_loop(0, PARTS, drain, 0)
+    def drain_back(p, carry):
+        wait_all(mid_return, p, sent.at[3, p])
+        return carry
+
+    lax.fori_loop(0, PARTS, drain_back, 0)
 
 
 def on_device(

time: 68.8 us -> 67.8 us (0.985)
  Pallas kernels: 67.8 us -> 66.9 us
    pallas_call x1, Pallas kernels: 67.8 us -> 66.9 us  [on_device(): pl.pallas_call(kernel, out_shape=pltpu.VMEM(tile, BF16), in_specs=[whole]...]
where the time goes in v6:
time: 67.8 us; the launch traced here: 67.7 us
  Pallas kernels  66.9 us (99%)
  local copies, waits for them, and re-layouts  0.8 us (1%)
    pallas_call x1, Pallas kernels, on_device(): pl.pallas_call(kernel, out_shape=pltpu.VMEM(tile, BF16), in_specs=[whole]...  66.9 us

profile of v6, /device:TPU:5, one launch (start us, length us, event | category | flops | bytes accessed | tf_op | source)
XLA Modules:
  0.0 67.7 jit_solution(8356902160257241807)
XLA Ops:
  0.0 66.9 %maxvit_layer.1 = bf16[2,8,32,512]{3,2,1,0:T(8,128)(2,1)S(1)} custom-call(bf16[2,8,32,512]{3,2,1,0:T(8,128)(2,1)} %x_hbm.1, f32[1,512]{1,0:T(1,128)} %bitcast.6, bf16[512,1024]{1,0:T(8,128)(2,1)} %we_hbm.1, f32[3,3,1024]{2,1,0:T(4,128)} %dw_hbm.1, f32[1,1024]{1,0:T(1,128)} %bitcast.5, bf16[1024,512]{1,0:T(8,128)(2,1)} %wp_hbm.1, f32[1,512]{1,0:T(1,128)} %bitcast.7, ...), custom_call_target="tpu_custom_call" | custom-call | tf_op jit(solution)/shard_map/maxvit_layer/pallas_call | solution.py:461
  66.9 0.8 %copy.12 = bf16[2,8,32,512]{3,2,1,0:T(8,128)(2,1)} copy(bf16[2,8,32,512]{3,2,1,0:T(8,128)(2,1)S(1)} %maxvit_layer.1) | data formatting | bytes 1048576

commit v7 on v6

--- a/solution.py
+++ b/solution.py
@@ -251,9 +251,6 @@
             att[p, rows] = layer_norm(conv[p, rows].astype(F32), gain).astype(BF16)
 
     convolve(0, True, 0)
-    pl.semaphore_wait(barrier, 2 * (SIDE - 1) + 6)
-    exchange(0, 0, att, mid, along_rows, a)
-
     loads[10].wait()
     place = iota((96, 1), 0)
     piece, index = place >> 4, place & 15
@@ -262,8 +259,11 @@
     cell_x = (piece & 1) * 31
     chosen = iota((96, 512), 1) == cell_f * CELLS + cell_y * COLS + cell_x
     edge[...] = matmul(one_hot(chosen), xb[...].reshape(512, WIDTH)).astype(BF16).reshape(6, 16, WIDTH)
+    pl.semaphore_wait(barrier, 2 * (SIDE - 1) + 6)
     for copy in halos:
         copy.start()
+    exchange(0, 0, att, mid, along_rows, a)
+
     expand_tile(1)
     convolve(1, True, 1)
     exchange(0, 1, att, mid, along_rows, a)

time: 67.8 us -> 66.1 us (0.975)
  the two profiles are of different devices: /device:TPU:5 before, /device:TPU:36 now
where the time goes in v7:
time: 66.1 us; the launch traced here: 66 us
  Pallas kernels  65.2 us (99%)
  local copies, waits for them, and re-layouts  0.8 us (1%)
    pallas_call x1, Pallas kernels, on_device(): pl.pallas_call(kernel, out_shape=pltpu.VMEM(tile, BF16), in_specs=[whole]...  65.2 us

profile of v7, /device:TPU:36, one launch (start us, length us, event | category | flops | bytes accessed | tf_op | source)
XLA Modules:
  0.0 66.0 jit_solution(12685991831253521207)
XLA Ops:
  0.0 65.2 %maxvit_layer.1 = bf16[2,8,32,512]{3,2,1,0:T(8,128)(2,1)S(1)} custom-call(bf16[2,8,32,512]{3,2,1,0:T(8,128)(2,1)} %x_hbm.1, f32[1,512]{1,0:T(1,128)} %bitcast.6, bf16[512,1024]{1,0:T(8,128)(2,1)} %we_hbm.1, f32[3,3,1024]{2,1,0:T(4,128)} %dw_hbm.1, f32[1,1024]{1,0:T(1,128)} %bitcast.5, bf16[1024,512]{1,0:T(8,128)(2,1)} %wp_hbm.1, f32[1,512]{1,0:T(1,128)} %bitcast.7, ...), custom_call_target="tpu_custom_call" | custom-call | tf_op jit(solution)/shard_map/maxvit_layer/pallas_call | solution.py:461
  65.2 0.8 %copy.12 = bf16[2,8,32,512]{3,2,1,0:T(8,128)(2,1)} copy(bf16[2,8,32,512]{3,2,1,0:T(8,128)(2,1)S(1)} %maxvit_layer.1) | data formatting | bytes 1048576
